TPU v7x, 256 devices: a whole 4x4x8 slice. The times are simulated.
256 devices in a mesh: group: 4 (over y), seq: 16 (over z, x_hi), mp: 4 (over x_lo, core).
Axes of the slice: x: 4 (x_hi: 2, x_lo: 2; x = x_hi * 2 + x_lo), y: 4, z: 8, core: 2. Of those that a mesh axis runs over, the one named last changes fastest.
Arguments:
- gen_input: bfloat16 [4096, 5120], P('seq'), may hold values from -22 to 22
- noise: bfloat16 [4096, 5120], P('seq'), may hold values from -22 to 22
- gen_steps: int32 [2], replicated, may hold values from 0 to 15
- critic_steps: int32 [2], replicated, may hold values from 0 to 15
- row_order: int32 [16, 256], P('seq'), may hold values from 0 to 255, each once within a row
- gen_wq: bfloat16 [5120, 2560], P('seq', 'mp'), may hold values from -0.078125 to 0.078125
- gen_wo: bfloat16 [5120, 2560], P('seq', 'mp'), may hold values from -0.125 to 0.125
- teacher_wq: bfloat16 [5120, 2560], P('seq', 'mp'), may hold values from -0.078125 to 0.078125
- teacher_wo: bfloat16 [5120, 2560], P('seq', 'mp'), may hold values from -0.125 to 0.125
- fake_wq: bfloat16 [5120, 2560], P('seq', 'mp'), may hold values from -0.078125 to 0.078125
- fake_wo: bfloat16 [5120, 2560], P('seq', 'mp'), may hold values from -0.125 to 0.125
- gen_mod: bfloat16 [16, 3, 5120], replicated, may hold values from -4 to 4
- teacher_mod: bfloat16 [16, 3, 5120], replicated, may hold values from -4 to 4
- fake_mod: bfloat16 [16, 3, 5120], replicated, may hold values from -4 to 4
- text_keys: bfloat16 [4, 512, 2560], P('group', None, 'mp'), may hold values from -6 to 6
- text_values: bfloat16 [4, 512, 2560], P('group', None, 'mp'), may hold values from -24 to 24
Outputs:
- predictions: bfloat16 [4, 4096, 5120], P('group', 'seq', 'mp')
- input_grads: float32 [4, 4096, 5120], P('group', 'seq', 'mp')
Inputs may be any that keep to these rules, and one draw needn't show every extreme that they name: `row_order`: each row lists the 256 positions of one block once each.
All inputs are finite; a program needn't handle non-finite values. Where the computation divides by a largest or mean magnitude, that divisor is 1e-20 or more.
Results may differ from a plain program's by a relative error of at most 0.038.
Values may be sent and summed in bfloat16 or wider, within the bound.
A program may use at most 128 MiB of HBM per device.

v0:
```python
import jax
import jax.numpy as jnp
from jax import lax
from jax.sharding import PartitionSpec as P

D = 5120
HEAD = 128
SAMPLES = 2
GROUPS = 4


EPSILON = 1e-06
FLOOR_EPSILON = 1e-05
GUIDANCE = 3.0


def spread(value, axis, root):
    mine = lax.axis_index(axis) == root
    return lax.psum(jnp.where(mine, value, jnp.zeros_like(value)), axis)


def head_norm(values, head_size):
    shaped = values.reshape(values.shape[0], -1, head_size)
    factor = lax.rsqrt(jnp.mean(shaped * shaped, axis=2, keepdims=True) + EPSILON)
    return (shaped, factor)


def attend(query_rows, keys_normed, value_cache, head_size):
    query_heads, query_scale = head_norm(query_rows, head_size)
    normed = (query_heads * query_scale).astype(jnp.bfloat16)
    key_heads = keys_normed.reshape(keys_normed.shape[0], -1, head_size)
    value_heads = value_cache.reshape(value_cache.shape[0], -1, head_size)
    scores = jnp.einsum(
        "nhd,thd->hnt", normed, key_heads, preferred_element_type=jnp.float32
    ) * head_size ** (-0.5)
    exponent = jnp.exp(scores)
    softmax_rows = (exponent / jnp.sum(exponent, axis=2, keepdims=True)).astype(jnp.bfloat16)
    mixed_rows = jnp.einsum(
        "hnt,thd->nhd", softmax_rows, value_heads, preferred_element_type=jnp.float32
    )
    return (
        mixed_rows.reshape(query_rows.shape[0], -1).astype(jnp.bfloat16),
        softmax_rows,
        query_heads,
        query_scale,
    )


def attend_back(
    grad_mixed, softmax_rows, query_heads, query_scale, keys_normed, value_cache, head_size
):
    count = grad_mixed.shape[0]
    key_heads = keys_normed.reshape(keys_normed.shape[0], -1, head_size)
    value_heads = value_cache.reshape(value_cache.shape[0], -1, head_size)
    grad_heads = grad_mixed.reshape(count, -1, head_size)
    grad_probs = jnp.einsum(
        "nhd,thd->hnt", grad_heads, value_heads, preferred_element_type=jnp.float32
    )
    weights = softmax_rows.astype(jnp.float32)
    grad_scores = (
        weights * (grad_probs - jnp.sum(weights * grad_probs, axis=2, keepdims=True))
    ).astype(jnp.bfloat16)
    grad_normed = jnp.einsum(
        "hnt,thd->nhd", grad_scores, key_heads, preferred_element_type=jnp.float32
    ) * head_size ** (-0.5)
    unit = query_heads * query_scale
    grad_query = query_scale * (
        grad_normed - unit * jnp.mean(unit * grad_normed, axis=2, keepdims=True)
    )
    return grad_query.reshape(count, -1).astype(jnp.bfloat16)


def sum_heads(partial_terms):
    return lax.psum(partial_terms.astype(jnp.bfloat16), "mp").astype(jnp.float32)


def modulate(input_rows, modulation):
    rows_float = input_rows.astype(jnp.float32)
    inverse = lax.rsqrt(jnp.mean(rows_float * rows_float, axis=1, keepdims=True) + EPSILON)
    hidden = (rows_float * inverse * (1.0 + modulation[1]) + modulation[0]).astype(jnp.bfloat16)
    return (rows_float, inverse, hidden)


def finish(rows_float, modulation, partial_terms):
    return (rows_float + modulation[2] * sum_heads(partial_terms)).astype(jnp.bfloat16)


def contract_last(left, right):
    return lax.dot_general(
        left, right, (((1,), (1,)), ((), ())), preferred_element_type=jnp.float32
    )


def on_device(
    gen_input,
    noise,
    gen_steps,
    critic_steps,
    row_order,
    gen_wq,
    gen_wo,
    teacher_wq,
    teacher_wo,
    fake_wq,
    fake_wo,
    gen_mod,
    teacher_mod,
    fake_mod,
    text_keys,
    text_values,
):
    head_size = HEAD
    group_index = lax.axis_index("group")
    seq_count = lax.axis_size("seq")
    mp_width = D // lax.axis_size("mp")
    mp_start = lax.axis_index("mp") * mp_width
    sample_index = lax.axis_index("seq") // (seq_count // SAMPLES)
    is_gen = group_index == 0
    is_fake = group_index == GROUPS - 1
    row_count = gen_input.shape[0]

    def chosen(first, middle, last):
        return jnp.where(is_gen, first, jnp.where(is_fake, last, middle))

    def own_cols(values):
        return lax.dynamic_slice_in_dim(values, mp_start, mp_width, values.ndim - 1)

    local_wq = chosen(gen_wq, teacher_wq, fake_wq)
    local_wo = chosen(gen_wo, teacher_wo, fake_wo)
    mod_table = chosen(gen_mod, teacher_mod, fake_mod).astype(jnp.float32)
    step_count = mod_table.shape[0]
    mod_flat = mod_table.reshape(step_count, -1)
    sample_ids = jnp.arange(SAMPLES, dtype=jnp.int32)

    def own_step(steps):
        return jnp.sum(jnp.where(sample_ids == sample_index, steps, 0))

    def lookup(steps):
        onehot = (jnp.arange(step_count, dtype=jnp.int32) == own_step(steps)).astype(jnp.float32)[
            None, :
        ]
        return jnp.dot(onehot, mod_flat, precision=lax.Precision.HIGHEST).reshape(3, -1)

    gen_modulation = lookup(gen_steps)
    critic_modulation = lookup(critic_steps)
    key_cache = text_keys[0]
    value_cache = text_values[0]
    key_heads, key_scale = head_norm(key_cache.astype(jnp.float32), head_size)
    keys_normed = (key_heads * key_scale).astype(jnp.bfloat16).reshape(key_cache.shape)
    floats_one, inverse_one, hidden_one = modulate(gen_input, gen_modulation)
    full_wq, full_wo = (
        lax.all_gather(local_wq, "seq", axis=0, tiled=True),
        lax.all_gather(local_wo, "seq", axis=0, tiled=True),
    )
    query_one = jnp.dot(hidden_one, full_wq, preferred_element_type=jnp.float32)
    mixed_one, softmax_one, qheads_one, qscale_one = attend(
        query_one, keys_normed, value_cache, head_size
    )
    terms_one = contract_last(mixed_one, full_wo)
    generated = finish(floats_one, gen_modulation, terms_one)
    relayed = spread(generated, "group", 0)
    local_order = row_order[0]
    arranged = jnp.take(relayed, local_order, axis=0)
    angle = 0.5 * jnp.pi * (own_step(critic_steps).astype(jnp.float32) + 1.0) / (step_count + 1.0)
    noised = (
        jnp.cos(angle) * arranged.astype(jnp.float32) + jnp.sin(angle) * noise.astype(jnp.float32)
    ).astype(jnp.bfloat16)
    floats_two, inverse_two, hidden_two = modulate(noised, critic_modulation)
    query_two = jnp.dot(hidden_two, full_wq, preferred_element_type=jnp.float32)
    mixed_two, softmax_two, qheads_two, qscale_two = attend(
        query_two, keys_normed, value_cache, head_size
    )
    terms_two = contract_last(mixed_two, full_wo)
    predicted = finish(floats_two, critic_modulation, terms_two)
    critic_slice = own_cols(predicted)
    prediction_slice = jnp.where(is_gen, own_cols(generated), critic_slice)
    every_role = lax.all_gather(critic_slice[None], "group", axis=0, tiled=True)
    cond = every_role[1].astype(jnp.float32)
    uncond = every_role[2].astype(jnp.float32)
    faked = every_role[3].astype(jnp.float32)
    real = GUIDANCE * cond - (GUIDANCE - 1.0) * uncond
    arranged_slice = own_cols(arranged).astype(jnp.float32)
    distance = jnp.sum(jnp.abs(arranged_slice - real))
    totals = lax.psum(jnp.where(sample_ids == sample_index, distance, 0.0), ("seq", "mp"))
    sample_size = float(row_count * seq_count // SAMPLES * D)
    denominator = (
        jnp.sum(jnp.where(sample_ids == sample_index, totals, 0.0)) / sample_size + FLOOR_EPSILON
    )
    score = (faked - real) / denominator
    inverse_order = (
        jnp.zeros((row_count,), jnp.int32)
        .at[local_order]
        .set(jnp.arange(row_count, dtype=jnp.int32))
    )
    gen_cotangent = jnp.take(score, inverse_order, axis=0)
    cotangent = jnp.where(
        is_gen,
        gen_cotangent,
        jnp.where(
            group_index == 1,
            -GUIDANCE * score,
            jnp.where(group_index == 2, (GUIDANCE - 1.0) * score, faked - arranged_slice),
        ),
    )
    rows_float = jnp.where(is_gen, floats_one, floats_two)
    inverse = jnp.where(is_gen, inverse_one, inverse_two)
    modulation = jnp.where(is_gen, gen_modulation, critic_modulation)
    softmax_rows = jnp.where(is_gen, softmax_one, softmax_two)
    query_heads = jnp.where(is_gen, qheads_one, qheads_two)
    query_scale = jnp.where(is_gen, qscale_one, qscale_two)
    gate_slice = own_cols(modulation[2])
    grad_slice = (gate_slice[None, :] * cotangent).astype(jnp.bfloat16)
    grad_out = lax.all_gather(grad_slice, "mp", axis=1, tiled=True)
    grad_mixed = jnp.dot(grad_out, full_wo, preferred_element_type=jnp.float32).astype(jnp.bfloat16)
    grad_query = attend_back(
        grad_mixed, softmax_rows, query_heads, query_scale, keys_normed, value_cache, head_size
    )
    grad_terms = contract_last(grad_query, full_wq)
    multiplier = 1.0 + modulation[1]
    grad_hidden = sum_heads(grad_terms)
    inner = jnp.mean(rows_float * multiplier * grad_hidden, axis=1, keepdims=True)
    full_term = inverse * multiplier * grad_hidden - rows_float * inverse**3 * inner
    term_slice = own_cols(full_term)
    input_slice = cotangent + term_slice
    return (prediction_slice[None], input_slice[None])


def solution(mesh):
    placed = (
        P("seq", None),
        P("seq", None),
        P(),
        P(),
        P("seq", None),
        P("seq", "mp"),
        P("seq", "mp"),
        P("seq", "mp"),
        P("seq", "mp"),
        P("seq", "mp"),
        P("seq", "mp"),
        P(),
        P(),
        P(),
        P("group", None, "mp"),
        P("group", None, "mp"),
    )
    return jax.shard_map(
        on_device,
        mesh=mesh,
        in_specs=placed,
        out_specs=(P("group", "seq", "mp"), P("group", "seq", "mp")),
        check_vma=False,
    )
```

profile of v0, /device:TPU:2, one launch (start us, length us, event | category | flops | bytes accessed | tf_op | source)
XLA Modules:
  0.0 814.9 jit_solution(6145487992981901385)
XLA Ops:
  13.8 2.2 copy.34
  18.4 112.9 %all-gather.6.cloned.1.call-done = bf16[5120,640]{1,0:T(8,128)(2,1)} async-done(((bf16[320,640]{1,0:T(8,128)(2,1)}), bf16[5120,640]{1,0:T(8,128)(2,1)}) %all-gather.6.cloned.1.call-update) | async-done | bytes 6553616 | tf_op jit(solution)/shard_map/all_gather | solution.py:152
  131.2 5.8 fusion.8
  140.7 108.2 %all-gather.8.cloned.1.call-done = bf16[5120,640]{1,0:T(8,128)(2,1)} async-done(((bf16[320,640]{1,0:T(8,128)(2,1)}), bf16[5120,640]{1,0:T(8,128)(2,1)}) %all-gather.8.cloned.1.call-update) | async-done | bytes 6553616 | tf_op jit(solution)/shard_map/all_gather | solution.py:153
  248.9 6.7 convolution_convert_fusion.2
  255.6 67.4 %all-reduce.5.cloned.1.call-done = bf16[256,5120]{1,0:T(8,128)(2,1)} async-done(((bf16[256,5120]{1,0:T(8,128)(2,1)}), bf16[256,5120]{1,0:T(8,128)(2,1)}) %all-reduce.5.cloned.1.call-update) | async-done | bytes 2621456 | tf_op jit(solution)/shard_map/psum | solution.py:74
  323.0 5.3 broadcast_select_fusion.1
  330.3 73.2 %all-reduce.7.cloned.1.call-done = bf16[256,5120]{1,0:T(8,128)(2,1)} async-done(((bf16[256,5120]{1,0:T(8,128)(2,1)}), bf16[256,5120]{1,0:T(8,128)(2,1)}) %all-reduce.7.cloned.1.call-update) | async-done | bytes 2621456 | tf_op jit(solution)/shard_map/psum | solution.py:19
  403.6 8.3 %gather_fusion = bf16[256,5120]{1,0:T(8,128)(2,1)} fusion(bf16[256,5120]{1,0:T(8,128)(2,1)} %all-reduce.7.cloned.1.call-done, s32[1024]{0:T(1024)S(1)} %pad_clamp_fusion.1), kind=kCustom, calls=%fused_computation | custom fusion | bytes 5243904 | tf_op jit(solution)/shard_map/jit(_take)/gather | solution.py:163
  411.9 5.2 multiply_reduce_fusion.1
  417.0 6.8 fusion.7
  426.8 3.8 convolution_convert_fusion.1
  430.7 2.9 convert_element_type.147
  433.6 66.3 %all-reduce.9.cloned.1.call-done = bf16[256,5120]{1,0:T(8,128)(2,1)} async-done(((bf16[256,5120]{1,0:T(8,128)(2,1)}), bf16[256,5120]{1,0:T(8,128)(2,1)}) %all-reduce.9.cloned.1.call-update) | async-done | bytes 2621456 | tf_op jit(solution)/shard_map/psum | solution.py:74
  499.9 3.0 select_bitcast_fusion
  504.5 39.1 %all-gather.12.cloned.1.call-done = bf16[1024,1280]{1,0:T(8,128)(2,1)} async-done(((bf16[256,1280]{1,0:T(8,128)(2,1)}), bf16[1024,1280]{1,0:T(8,128)(2,1)}) %all-gather.12.cloned.1.call-update) | async-done | bytes 2621456 | tf_op jit(solution)/shard_map/all_gather | solution.py:177
  543.6 2.5 fusion.19
  546.8 123.9 %psum.38 = f32[2]{0:T(128)S(1)} all-reduce(f32[2]{0:T(128)S(1)} %fusion.56), channel_id=1, replica_groups=mesh['group'=4,'seq'=16,'mp'=4] {'seq','mp'}, use_global_device_ids=true, to_apply=%region_14.15 | all-reduce | flops 2 | bytes 16 | tf_op jit(solution)/shard_map/psum | solution.py:184
  675.0 3.8 multiply_convert_fusion
  679.0 34.0 %all-gather.10.cloned.1.call-done = bf16[256,5120]{1,0:T(8,128)(2,1)} async-done(((bf16[256,1280]{1,0:T(8,128)(2,1)}), bf16[256,5120]{1,0:T(8,128)(2,1)}) %all-gather.10.cloned.1.call-update) | async-done | bytes 2621456 | tf_op jit(solution)/shard_map/all_gather | solution.py:213
  713.1 6.6 convolution_convert_fusion.3
  725.5 3.8 convolution_convert_fusion
  729.4 72.0 %all-reduce.11.cloned.1.call-done = bf16[256,5120]{1,0:T(8,128)(2,1)} async-done(((bf16[256,5120]{1,0:T(8,128)(2,1)}), bf16[256,5120]{1,0:T(8,128)(2,1)}) %all-reduce.11.cloned.1.call-update) | async-done | bytes 2621456 | tf_op jit(solution)/shard_map/psum | solution.py:74
  801.4 3.9 multiply_reduce_fusion
  (122 shorter events, 31.5 us)
Async XLA Ops:
  7.2 4.3 copy-start.18
  7.2 4.3 copy-start.19
  7.2 4.3 copy-start.17
  7.2 124.1 %all-gather.6.cloned.1.call-start = ((), (), s32[]{:S(2)}) async-start(), calls=%async_computation | async-start | bytes 6963200 | tf_op jit(solution)/shard_map/all_gather | solution.py:152
  9.3 239.5 %all-gather.8.cloned.1.call-start = ((), (), s32[]{:S(2)}) async-start(), calls=%async_computation.1 | async-start | bytes 6963200 | tf_op jit(solution)/shard_map/all_gather | solution.py:153
  11.4 311.6 %all-reduce.5.cloned.1.call-start = ((), (), s32[]{:S(2)}) async-start(), calls=%async_computation.2 | async-start | bytes 5242880 | tf_op jit(solution)/shard_map/psum | solution.py:74
  11.4 4.6 copy-start.21
  11.5 4.6 copy-start.22
  11.5 5.4 copy-start
  255.6 148.0 %all-reduce.7.cloned.1.call-start = ((), (), s32[]{:S(2)}) async-start(), calls=%async_computation.3 | async-start | bytes 5242880 | tf_op jit(solution)/shard_map/psum | solution.py:19
  328.3 171.6 %all-reduce.9.cloned.1.call-start = ((), (), s32[]{:S(2)}) async-start(), calls=%async_computation.4 | async-start | bytes 5242880 | tf_op jit(solution)/shard_map/psum | solution.py:74
  411.9 14.9 %slice-start.2 = ((s8[6553600]{0:T(1024)(128)(4,1)}), s8[4194304]{0:T(1024)(128)(4,1)S(1)}, s32[]{:S(2)}) async-start(s8[6553600]{0:T(1024)(128)(4,1)} %bitcast.83), calls=%async_computation.10 | async-start | bytes 8388608
  417.0 13.7 %copy-start.2 = (bf16[256,5120]{1,0:T(8,128)(2,1)}, bf16[256,5120]{1,0:T(8,128)(2,1)S(1)}, u32[]{:S(2)}) copy-start(bf16[256,5120]{1,0:T(8,128)(2,1)S(1)} %get-tuple-element.11) | copy-start | bytes 7864324
  417.0 9.7 %slice-start.3 = ((s8[6553600]{0:T(1024)(128)(4,1)}), s8[2359296]{0:T(1024)(128)(4,1)S(1)}, s32[]{:S(2)}) async-start(s8[6553600]{0:T(1024)(128)(4,1)} %bitcast.83), calls=%async_computation.11 | async-start | bytes 4718592
  430.6 113.0 %all-gather.12.cloned.1.call-start = ((), (), s32[]{:S(2)}) async-start(), calls=%async_computation.7 | async-start | bytes 3276800 | tf_op jit(solution)/shard_map/all_gather | solution.py:177
  502.9 210.1 %all-gather.10.cloned.1.call-start = ((), (), s32[]{:S(2)}) async-start(), calls=%async_computation.5 | async-start | bytes 3276800 | tf_op jit(solution)/shard_map/all_gather | solution.py:213
  678.7 42.8 %copy-start.4 = (bf16[5,256,512]{2,1,0:T(8,128)(2,1)S(1)}, bf16[5,256,512]{2,1,0:T(8,128)(2,1)}, u32[]{:S(2)}) copy-start(bf16[5,256,512]{2,1,0:T(8,128)(2,1)} %copy-done.3) | copy-start | bytes 3932164
  678.8 42.8 %copy-start.6 = (bf16[5,256,512]{2,1,0:T(8,128)(2,1)S(1)}, bf16[5,256,512]{2,1,0:T(8,128)(2,1)}, u32[]{:S(2)}) copy-start(bf16[5,256,512]{2,1,0:T(8,128)(2,1)} %copy-done.5) | copy-start | bytes 3932164
  678.8 122.6 %all-reduce.11.cloned.1.call-start = ((), (), s32[]{:S(2)}) async-start(), calls=%async_computation.6 | async-start | bytes 5242880 | tf_op jit(solution)/shard_map/psum | solution.py:74
  721.5 2.0 copy-start.8
  721.5 2.0 copy-start.10
  721.5 3.2 slice-start
  729.3 72.1 %copy-start.1 = (bf16[256,5120]{1,0:T(8,128)(2,1)S(1)}, bf16[256,5120]{1,0:T(8,128)(2,1)}, u32[]{:S(2)}) copy-start(bf16[256,5120]{1,0:T(8,128)(2,1)} %param.16) | copy-start | bytes 7864324
  801.4 4.0 copy-start.11
  (11 other events, 14.8 us)
Sparse Core Ops, SparseCore 0:
  11.2 120.0 all-gather.5
  133.8 114.9 all-gather.7
  255.7 67.2 all-reduce.4
  328.4 75.0 all-reduce.6
  430.7 69.1 all-reduce.8
  503.1 40.4 all-gather.11
  678.9 34.1 all-gather.9
  729.4 71.9 all-reduce.10
where the time goes:
time: 818 us; the launch traced here: 815 us
  waiting for transfers between devices  573 us (70%)
  blocking collectives  124 us (15%)
  matrix products  41.3 us (5%)
  other arithmetic  38.5 us (5%)
  local copies, waits for them, and re-layouts  21.2 us (3%)
  between operations  16.2 us (2%)
    psum x3, waiting for transfers between devices, sum_heads(): lax.psum(partial_terms.astype(jnp.bfloat16), 'mp').astype(jnp.float32)  206 us
    psum x1, blocking collectives, on_device(): lax.psum(jnp.where(sample_ids == sample_index, distance, 0.0), ('seq', 'm...  124 us
    all_gather x1, waiting for transfers between devices, on_device(): lax.all_gather(local_wq, 'seq', axis=0, tiled=True)  113 us
    all_gather x1, waiting for transfers between devices, on_device(): lax.all_gather(local_wo, 'seq', axis=0, tiled=True)  108 us
    psum x1, waiting for transfers between devices, spread(): return lax.psum(jnp.where(mine, value, jnp.zeros_like(value)), axis)  73.2 us
    all_gather x1, waiting for transfers between devices, on_device(): every_role = lax.all_gather(critic_slice[None], 'group', axis=0, tiled=True)  39.1 us
    all_gather x1, waiting for transfers between devices, on_device(): grad_out = lax.all_gather(grad_slice, 'mp', axis=1, tiled=True)  34 us
  transfers between devices with their start and end apart: 8, of which 8 were waited for; matrix products, arithmetic and copies ran while one was open for 3% of the time, Pallas kernels for 0%

commit v1 on v0

v1 whole, which is shorter than its diff:
```python
import jax
import jax.numpy as jnp
from jax import lax
from jax.experimental import pallas as pl
from jax.experimental.pallas import tpu as pltpu
from jax.sharding import PartitionSpec as P

D = 5120
HEAD = 128
SAMPLES = 2
GROUPS = 4
TOK = 256
TEXT = 512
COLS = 640
HEADS = 5
SUB = 80
SLICE = 320
QUARTER = 1280
QROWS = TOK + 16
QCOLS = COLS + 128
LAG = 3
EPSILON = 1e-06
FLOOR_EPSILON = 1e-05
GUIDANCE = 3.0
BF = jnp.bfloat16
F32 = jnp.float32

GQ, GO, TQ, FQ, TO, FO = range(6)


def dot_nn(a, b):
    return lax.dot_general(a, b, (((1,), (0,)), ((), ())), preferred_element_type=F32)


def dot_nt(a, b):
    return lax.dot_general(a, b, (((1,), (1,)), ((), ())), preferred_element_type=F32)


def dot_tn(a, b):
    return lax.dot_general(a, b, (((0,), (0,)), ((), ())), preferred_element_type=F32)


class Slots:
    def __init__(self):
        self.count = 0

    def take(self, number):
        first = self.count
        self.count += number
        return first


SLOTS = Slots()
RING = SLOTS.take(2 * 6 * 7)
XCH = SLOTS.take(6)
YQG = SLOTS.take(4)
YQC = SLOTS.take(4)
YMG = SLOTS.take(4)
YMC = SLOTS.take(4)
YPR = SLOTS.take(4)
YGN = SLOTS.take(4)
YNO = SLOTS.take(4)
YCO = SLOTS.take(4)
YGM = SLOTS.take(4)
YGQ = SLOTS.take(4)
YGH = SLOTS.take(4)
YDI = SLOTS.take(4)
RSC = SLOTS.take(8 * 2)
RSX = SLOTS.take(8)
AGM = SLOTS.take(4 * 3)
BUT = SLOTS.take(5)
INN = SLOTS.take(2)
N_SEM = SLOTS.count


def kernel(
    wown, a1, x1s, nzs, onehot, shifts, cols, scols, r1, keys, values,
    out4, ss_out, inner_out, dist_out,
    W, qsg, qsc, qbuf, qA, qq, probs, mb, PP, CC, SS, XX, G, an,
    send_p, send_c, send_h, gms, gmb, gq, isend, irecv, dsend, drecv,
    ssem, rsem,
):
    g = lax.axis_index("group")
    s = lax.axis_index("seq")
    m = lax.axis_index("mp")
    z, xh = s // 2, lax.rem(s, 2)
    xl, c = m // 2, lax.rem(m, 2)
    m_core = 2 * xl + 1 - c
    m_x = 2 * (1 - xl) + c
    s_x = 2 * z + 1 - xh
    z_pair = z + 1 - 2 * lax.rem(z, 2)
    z_far = z + 2 - 4 * lax.rem(z // 2, 2)
    s_up = lax.rem(z + 1, 8) * 2 + xh
    s_down = lax.rem(z + 7, 8) * 2 + xh
    s_pair = z_pair * 2 + xh
    s_far = z_far * 2 + xh
    others = [lax.rem(g + k, GROUPS) for k in (1, 2, 3)]
    pending = []

    def rdma(src, dst, send, recv, **where):
        return pltpu.make_async_remote_copy(
            src_ref=src, dst_ref=dst, send_sem=ssem.at[send], recv_sem=rsem.at[recv],
            device_id=where, device_id_type=pl.DeviceIdType.MESH,
        )

    def start(copy):
        copy.start()
        pending.append(copy)

    barrier = pltpu.get_barrier_semaphore()
    peers = [{"group": o} for o in others]
    peers += [{"mp": m_core}, {"mp": m_x}, {"seq": s_x}, {"seq": s_up}, {"seq": s_down}, {"seq": s_far}]
    for peer in peers:
        pl.semaphore_signal(barrier, inc=1, device_id=peer, device_id_type=pl.DeviceIdType.MESH)
    pl.semaphore_wait(barrier, len(peers))

    def rows_of(zz, x):
        return pl.ds(pl.multiple_of((lax.rem(zz + 16, 8) * 2 + x) * SUB, 16), SUB)

    def ring_copy(way, k, t):
        sem = RING + (way * 6 + k) * 7 + t
        if way == 0:
            rows = rows_of(z - t, xh)
            src = wown.at[k] if t == 0 else W.at[k, rows]
            return rdma(src, W.at[k, rows], sem, sem, seq=s_up)
        rows = rows_of(z + t, 1 - xh)
        return rdma(W.at[k, rows], W.at[k, rows], sem, sem, seq=s_down)

    def ring_wait(way, k, t):
        sem = RING + (way * 6 + k) * 7 + t
        rows = rows_of(z - 1 - t, xh) if way == 0 else rows_of(z + 1 + t, 1 - xh)
        rdma(W.at[k, rows], W.at[k, rows], sem, sem, seq=s_up).wait_recv()

    my_rows = rows_of(z, xh)
    for k in range(6):
        start(rdma(wown.at[k], W.at[k, my_rows], XCH + k, XCH + k, seq=s_x))
    for k in range(6):
        W[k, my_rows, :] = wown[k]

    state = {"tick": 0}

    def ring_to(last):
        while state["tick"] <= last:
            tick = state["tick"]
            for k in range(6):
                t = tick - LAG * k
                if t == 0:
                    start(ring_copy(0, k, 0))
                    other = rows_of(z, 1 - xh)
                    rdma(W.at[k, other], W.at[k, other], XCH + k, XCH + k, seq=s_x).wait_recv()
                    start(ring_copy(1, k, 0))
            for k in range(6):
                t = tick - LAG * k
                if 0 <= t <= 6:
                    for way in (0, 1):
                        ring_wait(way, k, t)
                        if t < 6:
                            start(ring_copy(way, k, t + 1))
            state["tick"] += 1

    def have(k):
        ring_to(LAG * k + 6)

    def y_send(base, dg, src, dst):
        start(rdma(src, dst, base + dg, base + g, group=others[dg - 1]))

    def y_wait(base, source, ref):
        rdma(ref, ref, base, base + source, group=others[0]).wait_recv()

    def slice_rows(index):
        return pl.ds(pl.multiple_of(index * SLICE, 16), SLICE)

    def rs_first(r):
        for far in (1, 0):
            x = 1 - xl if far else xl
            start(rdma(PP.at[r, slice_rows(2 * x + 1 - c)], CC.at[r, x],
                       RSC + 2 * r + far, RSC + 2 * r + x, mp=m_core))

    def rs_core_wait(r, x):
        rdma(CC.at[r, x], CC.at[r, x], RSC + 2 * r, RSC + 2 * r + x, mp=m_core).wait_recv()

    def rs_second(r):
        rs_core_wait(r, 1 - xl)
        SS[r] = (PP[r, slice_rows(2 * (1 - xl) + c), :].astype(F32) + CC[r, 1 - xl].astype(F32)).astype(BF)
        start(rdma(SS.at[r], XX.at[r], RSX + r, RSX + r, mp=m_x))

    def rs_total(r):
        rs_core_wait(r, xl)
        rdma(XX.at[r], XX.at[r], RSX + r, RSX + r, mp=m_x).wait_recv()
        return (PP[r, slice_rows(m), :].astype(F32) + CC[r, xl].astype(F32)) + XX[r].astype(F32)

    def ag_first(r):
        rows = slice_rows(m)
        start(rdma(G.at[r, rows], G.at[r, rows], AGM + 3 * r, AGM + 3 * r, mp=m_x))
        start(rdma(G.at[r, rows], G.at[r, rows], AGM + 3 * r + 1, AGM + 3 * r + 1, mp=m_core))

    def ag_second(r):
        rows = slice_rows(m_x)
        rdma(G.at[r, rows], G.at[r, rows], AGM + 3 * r, AGM + 3 * r, mp=m_x).wait_recv()
        start(rdma(G.at[r, rows], G.at[r, rows], AGM + 3 * r + 2, AGM + 3 * r + 2, mp=m_core))

    def ag_wait(r):
        for extra, index in ((1, m_core), (2, 2 * (1 - xl) + 1 - c)):
            rows = slice_rows(index)
            rdma(G.at[r, rows], G.at[r, rows], AGM + 3 * r + extra, AGM + 3 * r + extra, mp=m_core).wait_recv()

    def planes(r, k, ref):
        def body(i, carry):
            rows = slice_rows(i)
            PP[r, rows, :] = dot_nt(W[k, rows, :], ref[...]).astype(BF)
            return carry
        lax.fori_loop(0, 4, body, 0)

    scaling = HEAD ** -0.5

    def lanes_of(h):
        return pl.ds(pl.multiple_of(h * HEAD, HEAD), HEAD)

    def attend(r, total, bias):
        qA[...] = total
        qq[...] = r * total + bias

        def head(h, carry):
            lanes = lanes_of(h)
            qh = qq[:, lanes]
            rq = lax.rsqrt(jnp.mean(qh * qh, axis=1, keepdims=True) + EPSILON)
            e = jnp.exp(dot_nt((qh * rq).astype(BF), keys[:, lanes]) * scaling)
            p = (e * (1.0 / jnp.sum(e, axis=1, keepdims=True))).astype(BF)
            probs[h] = p
            mb[g, :, lanes] = dot_nn(p, values[:, lanes]).astype(BF)
            return carry

        lax.fori_loop(0, HEADS, head, 0)

    def gathered(own):
        parts = [own] + [qbuf.at[o] for o in others]
        total = sum(p[0:TOK, 0:COLS].astype(F32) for p in parts)
        bias = sum(p[TOK:QROWS, 0:COLS].astype(F32) for p in parts)[0:1, :]
        extra = sum(p[0:TOK, COLS:QCOLS].astype(F32) for p in parts)
        return total, bias, extra

    def to_bf_rows(ref, part, bias, extra):
        ref[0:TOK, 0:COLS] = part.astype(BF)
        ref[TOK:QROWS, 0:COLS] = bias.astype(BF)
        ref[0:TOK, COLS:QCOLS] = extra
        ref[TOK:QROWS, COLS:QCOLS] = jnp.zeros((16, 128), BF)

    have(GQ)
    to_bf_rows(qsg, dot_tn(a1[...], W[GQ]), dot_nn(shifts[0], W[GQ]), jnp.zeros((TOK, 128), BF))
    gen_q = rdma(qsg, qbuf.at[g], YQG, YQG + g, group=0)

    @pl.when(g != 0)
    def _():
        gen_q.start()

    have(GO)

    gen_m = [rdma(mb.at[0], mb.at[0], YMG + k, YMG, group=others[k - 1]) for k in (1, 2, 3)]

    @pl.when(g == 0)
    def _():
        for o in others:
            y_wait(YQG, o, qbuf.at[o])
        total, bias, _ = gathered(qsg)
        attend(r1[...], total, bias)
        for copy in (gen_m[1], gen_m[0], gen_m[2]):
            copy.start()

    ring_to(LAG * TQ + 6)

    @pl.when(g != 0)
    def _():
        y_wait(YMG, 0, mb.at[0])

    planes(0, GO, mb.at[0])
    rs_first(0)
    rs_second(0)
    total = rs_total(0)
    gate_g, gate_t, gate_f = scols[:, 0:1], scols[:, 1:2], scols[:, 2:3]
    alpha, sigma = scols[:, 3:4], scols[:, 4:5]
    gen_s = (x1s[...].astype(F32) + gate_g * total).astype(BF)
    send_p[0] = gen_s
    arr = dot_nn(gen_s, onehot[...])
    noised = (alpha * arr + sigma * nzs[...].astype(F32)).astype(BF)
    G[0, slice_rows(m), :] = noised
    ag_first(0)
    ag_second(0)
    ag_wait(0)

    nf = G[0].astype(F32)
    sq = (nf * nf).astype(BF)
    squares = dot_tn(sq, jnp.ones((QUARTER, 128), BF))
    high = squares.astype(BF)
    low = (squares - high.astype(F32)).astype(BF)
    lane = lax.broadcasted_iota(jnp.int32, (TOK, 128), 1)
    extra = jnp.where(lane < 64, high.astype(F32), low.astype(F32)).astype(BF)
    an[0] = (nf * cols[:, 0:1]).astype(BF)
    an[1] = (nf * cols[:, 1:2]).astype(BF)
    have(TQ)
    to_bf_rows(qsc.at[0], dot_tn(an[0], W[TQ]), dot_nn(shifts[1], W[TQ]), extra)
    have(FQ)
    to_bf_rows(qsc.at[1], dot_tn(an[1], W[FQ]), dot_nn(shifts[2], W[FQ]), extra)
    crit_q = []
    for k in (2, 1, 3):
        t = others[k - 1]
        crit_q.append((t, rdma(qsc.at[t // 3], qbuf.at[g], YQC + k, YQC + g, group=t)))
    for t, copy in crit_q:
        @pl.when(t != 0)
        def _():
            copy.start()

    have(TO)
    crit_m = [rdma(mb.at[g], mb.at[g], YMC + k, YMC + g, group=others[k - 1]) for k in (1, 2, 3)]

    @pl.when(g != 0)
    def _():
        for o in others:
            y_wait(YQC, o, qbuf.at[o])
        total, bias, extra = gathered(qsc.at[g // 3])
        square = extra[:, 0:1] + extra[:, 64:65]
        r = lax.rsqrt(square * (1.0 / D) + EPSILON)
        ss_out[...] = jnp.broadcast_to(r, (TOK, 128))
        attend(r, total, bias)
        for copy in (crit_m[1], crit_m[0], crit_m[2]):
            copy.start()

    @pl.when(g == 0)
    def _():
        ss_out[...] = jnp.broadcast_to(r1[...], (TOK, 128))

    have(FO)
    for r in (1, 2, 3):
        @pl.when(g != r)
        def _():
            y_wait(YMC, r, mb.at[r])
        planes(r, TO if r < 3 else FO, mb.at[r])
        rs_first(r)
    for k in (2, 1, 3):
        y_send(YNO, k, G.at[0, slice_rows(m)], out4.at[2, g])
    gen_p = rdma(send_p.at[0], out4.at[0, g], YGN, YGN + g, group=0)

    @pl.when(g != 0)
    def _():
        gen_p.start()

    for r in (1, 2, 3):
        rs_second(r)
    own_n = G[0, slice_rows(m), :].astype(F32)
    for r in (1, 2, 3):
        gate = gate_t if r < 3 else gate_f
        send_p[r] = (own_n + gate * rs_total(r)).astype(BF)
    crit_p = []
    for k in (2, 1, 3):
        t = others[k - 1]
        crit_p.append((t, rdma(send_p.at[t], out4.at[0, g], YPR + k, YPR + g, group=t)))

    cond, uncond, faked = [send_p[r].astype(F32) for r in (1, 2, 3)]
    real = GUIDANCE * cond - (GUIDANCE - 1.0) * uncond
    score = faked - real
    score_b = score.astype(BF)
    gen_cot = dot_nt(score_b, onehot[...])
    send_c[0] = gen_cot.astype(BF)
    send_c[1] = score_b
    send_c[2] = score_b
    fake_cot = faked - arr
    send_c[3] = fake_cot.astype(BF)
    mine = slice_rows(m)
    G[1, mine, :] = (gate_g * gen_cot).astype(BF)
    ag_first(1)
    G[2, mine, :] = (gate_t * score).astype(BF)
    ag_first(2)
    G[3, mine, :] = (gate_f * fake_cot).astype(BF)
    ag_first(3)
    dist = jnp.sum(jnp.abs(arr - real), axis=0, keepdims=True)
    dist = dist[:, 0:128] + dist[:, 128:256]
    dsend[0] = jnp.broadcast_to(dist, (8, 128))
    for t, copy in crit_p:
        @pl.when(t != 0)
        def _():
            copy.start()

    def butterfly(step):
        where = [dict(mp=m_core), dict(mp=m_x), dict(seq=s_x), dict(seq=s_pair), dict(seq=s_far)][step]
        return rdma(dsend.at[step], drecv.at[step], BUT + step, BUT + step, **where)

    def butterfly_end(step):
        rdma(drecv.at[step], drecv.at[step], BUT + step, BUT + step, mp=m_core).wait_recv()
        dsend[step + 1] = dsend[step] + drecv[step]

    start(butterfly(0))
    for r in (1, 2, 3):
        ag_second(r)
    for r, k in ((1, GO), (2, TO), (3, FO)):
        ag_wait(r)
        gms[r - 1] = dot_tn(G[r], W[k]).astype(BF)
    for k in (2, 1, 3):
        t = others[k - 1]
        y_send(YGM, k, gms.at[(t + 1) // 2], gmb.at[g])
    butterfly_end(0)
    start(butterfly(1))

    for o in others:
        y_wait(YGM, o, gmb.at[o])
    total = gms[(g + 1) // 2].astype(F32)
    for o in others:
        total = total + gmb[o].astype(F32)
    factor = jnp.where(g == 1, -GUIDANCE, jnp.where(g == 2, GUIDANCE - 1.0, 1.0)).astype(F32)
    gmb[g] = (total * factor).astype(BF)

    def head_back(h, inner):
        lanes = lanes_of(h)
        qh = qq[:, lanes]
        rq = lax.rsqrt(jnp.mean(qh * qh, axis=1, keepdims=True) + EPSILON)
        unit = qh * rq
        w = probs[h].astype(F32)
        dp = dot_nt(gmb[g, :, lanes], values[:, lanes])
        gs = (w * (dp - jnp.sum(w * dp, axis=1, keepdims=True))).astype(BF)
        dqn = dot_nn(gs, keys[:, lanes]) * scaling
        grad = rq * (dqn - unit * jnp.mean(unit * dqn, axis=1, keepdims=True))
        gq[g, :, lanes] = grad.astype(BF)
        return inner + jnp.sum(grad * qA[:, lanes], axis=1, keepdims=True)

    inner = lax.fori_loop(0, HEADS, head_back, jnp.zeros((TOK, 1), F32))
    for k in (2, 1, 3):
        y_send(YGQ, k, gq.at[g], gq.at[g])
    isend[0] = jnp.broadcast_to(inner, (TOK, 128))
    start(rdma(isend.at[0], irecv.at[0], INN, INN, mp=m_core))
    butterfly_end(1)
    start(butterfly(2))
    rdma(irecv.at[0], irecv.at[0], INN, INN, mp=m_core).wait_recv()
    isend[1] = isend[0] + irecv[0]
    start(rdma(isend.at[1], irecv.at[1], INN + 1, INN + 1, mp=m_x))
    butterfly_end(2)
    start(butterfly(3))

    for r in range(4):
        @pl.when(g != r)
        def _():
            y_wait(YGQ, r, gq.at[r])
        planes(4 + r, (GQ, TQ, TQ, FQ)[r], gq.at[r])
        rs_first(4 + r)
    butterfly_end(3)
    start(butterfly(4))
    for r in range(4):
        rs_second(4 + r)
    for k in (2, 1, 3):
        t = others[k - 1]
        y_send(YCO, k, send_c.at[t], out4.at[1, g])
    for r in range(4):
        send_h[r] = rs_total(4 + r).astype(BF)
    for k in (2, 1, 3):
        t = others[k - 1]
        y_send(YGH, k, send_h.at[t], out4.at[3, g])
    butterfly_end(4)
    for k in (2, 1, 3):
        y_send(YDI, k, dsend.at[5], drecv.at[5 + g])
    rdma(irecv.at[1], irecv.at[1], INN + 1, INN + 1, mp=m_x).wait_recv()
    inner_out[...] = isend[1] + irecv[1]
    out4[0, g] = send_p[g]
    out4[1, g] = send_c[g]
    out4[2, g] = G[0, mine, :]
    out4[3, g] = send_h[g]
    total = dsend[5]
    for o in others:
        y_wait(YDI, o, drecv.at[5 + o])
        total = total + drecv[5 + o]
    dist_out[...] = total

    for o in others:
        y_wait(YNO, o, out4.at[2, o])
        y_wait(YCO, o, out4.at[1, o])
        y_wait(YGH, o, out4.at[3, o])

    @pl.when(g == 0)
    def _():
        for o in others:
            y_wait(YGN, o, out4.at[0, o])
        for copy in gen_m:
            copy.wait_send()

    @pl.when(g != 0)
    def _():
        for o in others:
            y_wait(YPR, o, out4.at[0, o])
        gen_q.wait_send()
        gen_p.wait_send()
        for copy in crit_m:
            copy.wait_send()

    for t, copy in crit_q + crit_p:
        @pl.when(t != 0)
        def _():
            copy.wait_send()

    for copy in pending:
        copy.wait_send()


def fused(*operands):
    vmem = pl.BlockSpec(memory_space=pltpu.VMEM)
    act = lambda *lead: pltpu.VMEM(lead + (SLICE, TOK), BF)
    return pl.pallas_call(
        kernel,
        out_shape=[
            jax.ShapeDtypeStruct((4, 4, SLICE, TOK), BF),
            jax.ShapeDtypeStruct((TOK, 128), F32),
            jax.ShapeDtypeStruct((TOK, 128), F32),
            jax.ShapeDtypeStruct((8, 128), F32),
        ],
        in_specs=[vmem] * len(operands),
        out_specs=[vmem] * 4,
        scratch_shapes=[
            pltpu.VMEM((6, QUARTER, COLS), BF),
            pltpu.VMEM((QROWS, QCOLS), BF),
            pltpu.VMEM((2, QROWS, QCOLS), BF),
            pltpu.VMEM((4, QROWS, QCOLS), BF),
            pltpu.VMEM((TOK, COLS), F32),
            pltpu.VMEM((TOK, COLS), F32),
            pltpu.VMEM((HEADS, TOK, TEXT), BF),
            pltpu.VMEM((4, TOK, COLS), BF),
            pltpu.VMEM((8, QUARTER, TOK), BF),
            act(8, 2),
            act(8),
            act(8),
            pltpu.VMEM((4, QUARTER, TOK), BF),
            pltpu.VMEM((2, QUARTER, TOK), BF),
            act(4),
            act(4),
            act(4),
            pltpu.VMEM((3, TOK, COLS), BF),
            pltpu.VMEM((4, TOK, COLS), BF),
            pltpu.VMEM((4, TOK, COLS), BF),
            pltpu.VMEM((2, TOK, 128), F32),
            pltpu.VMEM((2, TOK, 128), F32),
            pltpu.VMEM((6, 8, 128), F32),
            pltpu.VMEM((9, 8, 128), F32),
            pltpu.SemaphoreType.DMA((N_SEM,)),
            pltpu.SemaphoreType.DMA((N_SEM,)),
        ],
        compiler_params=pltpu.CompilerParams(
            collective_id=0, has_side_effects=True, vmem_limit_bytes=60 * 2**20
        ),
        cost_estimate=pl.CostEstimate(flops=8 * 10**9, bytes_accessed=10**7, transcendentals=10**6),
    )(*operands)


def on_device(
    gen_input, noise, gen_steps, critic_steps, row_order,
    gen_wq, gen_wo, teacher_wq, teacher_wo, fake_wq, fake_wo,
    gen_mod, teacher_mod, fake_mod, text_keys, text_values,
):
    g = lax.axis_index("group")
    s = lax.axis_index("seq")
    m = lax.axis_index("mp")
    sample = s // (lax.axis_size("seq") // SAMPLES)
    is_gen = g == 0
    is_fake = g == GROUPS - 1
    step_count = gen_mod.shape[0]

    def pick(values, index, axis):
        return lax.dynamic_index_in_dim(values, index, axis, keepdims=False)

    def quarter(values):
        return pick(values.reshape(values.shape[:-1] + (16, 4, SUB)), g, values.ndim).reshape(
            values.shape[:-1] + (QUARTER,)
        )

    def own_slice(values):
        return lax.dynamic_slice_in_dim(values, m * SLICE, SLICE, values.ndim - 1)

    def block(values):
        return lax.dynamic_slice_in_dim(values, m * QUARTER, QUARTER, values.ndim - 1)

    gen_step = pick(gen_steps, sample, 0)
    critic_step = pick(critic_steps, sample, 0)
    mod_g = pick(gen_mod, gen_step, 0).astype(F32)
    mod_t = pick(teacher_mod, critic_step, 0).astype(F32)
    mod_f = pick(fake_mod, critic_step, 0).astype(F32)
    quarter_g, quarter_t, quarter_f = quarter(mod_g), quarter(mod_t), quarter(mod_f)

    x = gen_input.astype(F32)
    r1 = lax.rsqrt(jnp.mean(x * x, axis=1, keepdims=True) + EPSILON)
    xq = quarter(gen_input)
    a1 = (xq.astype(F32) * (1.0 + quarter_g[1])).astype(BF).T
    x1s = own_slice(xq).T
    nzs = own_slice(quarter(noise)).T
    order = row_order[0]
    onehot = (jnp.arange(TOK, dtype=jnp.int32)[:, None] == order[None, :]).astype(BF)
    shifts = jnp.broadcast_to(
        jnp.stack([quarter_g[0], quarter_t[0], quarter_f[0]])[:, None, :], (3, 16, QUARTER)
    ).astype(BF)
    angle = 0.5 * jnp.pi * (critic_step.astype(F32) + 1.0) / (step_count + 1.0)
    cols = jnp.stack([1.0 + quarter_t[1], 1.0 + quarter_f[1]], axis=1)
    ones = jnp.ones((SLICE,), F32)
    scols = jnp.stack(
        [own_slice(quarter_g[2]), own_slice(quarter_t[2]), own_slice(quarter_f[2]),
         ones * jnp.cos(angle), ones * jnp.sin(angle)], axis=1)
    wown = jnp.stack([
        lax.dynamic_slice_in_dim(w, g * SUB, SUB, 0)
        for w in (gen_wq, gen_wo, teacher_wq, fake_wq, teacher_wo, fake_wo)
    ])
    kf = text_keys[0].astype(F32).reshape(TEXT, HEADS, HEAD)
    keys = (kf * lax.rsqrt(jnp.mean(kf * kf, axis=2, keepdims=True) + EPSILON)).astype(BF)
    keys = keys.reshape(TEXT, COLS)

    out4, r_cols, inner_cols, dist = fused(
        wown, a1, x1s, nzs, onehot, shifts, cols, scols, r1, keys, text_values[0]
    )
    rows = out4.reshape(4, 4, 4, SUB, TOK).transpose(0, 4, 2, 1, 3).reshape(4, TOK, QUARTER)
    predictions = rows[0]
    cot, noised, grad_hidden = rows[1].astype(F32), rows[2].astype(F32), rows[3].astype(F32)
    r = r_cols[:, 0:1]
    inner = inner_cols[:, 0:1] * (1.0 / D)
    sample_size = float(TOK * lax.axis_size("seq") // SAMPLES * D)
    denominator = jnp.sum(dist[0]) / sample_size + FLOOR_EPSILON
    scale = block(jnp.where(is_gen, mod_g[1], jnp.where(is_fake, mod_f[1], mod_t[1])))
    x_rows = jnp.where(is_gen, block(x), noised)
    factor = jnp.where(g == 1, -GUIDANCE, jnp.where(g == 2, GUIDANCE - 1.0, 1.0))
    grads = factor * cot + r * (1.0 + scale) * grad_hidden - x_rows * (r * r * r * inner)
    grads = grads * jnp.where(is_fake, 1.0, 1.0 / denominator)
    return (predictions[None], grads[None])


def solution(mesh):
    placed = (
        P("seq", None),
        P("seq", None),
        P(),
        P(),
        P("seq", None),
        P("seq", "mp"),
        P("seq", "mp"),
        P("seq", "mp"),
        P("seq", "mp"),
        P("seq", "mp"),
        P("seq", "mp"),
        P(),
        P(),
        P(),
        P("group", None, "mp"),
        P("group", None, "mp"),
    )
    return jax.shard_map(
        on_device,
        mesh=mesh,
        in_specs=placed,
        out_specs=(P("group", "seq", "mp"), P("group", "seq", "mp")),
        check_vma=False,
    )
```

time: 818 us -> 298 us (0.36)
  waiting for transfers between devices: 573 us -> 0 us
  Pallas kernels: 0 us -> 248 us
  blocking collectives: 124 us -> 0 us
  matrix products: 41.3 us -> 0 us
  other arithmetic: 38.5 us -> 11.8 us
  between operations: 16.2 us -> 6.33 us
  local copies, waits for them, and re-layouts: 21.2 us -> 30.8 us
    all_gather x4 -> x0, waiting for transfers between devices: 294 us -> none  [the longest x1 113 us: on_device(): lax.all_gather(local_wq, 'seq', axis=0, tiled=True)]
    psum x4 -> x0, waiting for transfers between devices: 279 us -> none  [the longest x3 206 us: sum_heads(): lax.psum(partial_terms.astype(jnp.bfloat16), 'mp').astype(jnp.float32)]
    pallas_call x0 -> x1, Pallas kernels: none -> 248 us  [fused(): pl.pallas_call(kernel, out_shape=[jax.ShapeDtypeStruct((4, 4, SLICE, TOK)...]
    psum x1 -> x0, blocking collectives: 124 us -> none  [on_device(): lax.psum(jnp.where(sample_ids == sample_index, distance, 0.0), ('seq', 'm...]
    dot_general x14 -> x0, matrix products: 41.3 us -> none  [the longest x3 14.2 us: contract_last(): lax.dot_general(left, right, (((1,), (1,)), ((), ())), preferred_element_...]
    reduce_sum x9 -> x3, other arithmetic: 13.7 us -> 2.12 us  [the longest x1 1.29 us: on_device(): denominator = jnp.sum(dist[0]) / sample_size + FLOOR_EPSILON]
    select_n x8 -> x0, other arithmetic: 10 us -> none  [the longest x1 5.33 us: spread(): return lax.psum(jnp.where(mine, value, jnp.zeros_like(value)), axis)]
    gather x2 -> x0, local copies, waits for them, and re-layouts: 9.5 us -> none  [the longest x1 8.28 us: on_device(): arranged = jnp.take(relayed, local_order, axis=0)]
  transfers between devices with their start and end apart: 8 -> 0, of which waited for: 8 -> 0; matrix products, arithmetic and copies ran while one was open for 3% -> 0% of each run, Pallas kernels for 0% -> 0%
where the time goes in v1:
time: 298 us; the launch traced here: 297 us
  Pallas kernels  248 us (83%)
  local copies, waits for them, and re-layouts  30.8 us (10%)
  other arithmetic  11.8 us (4%)
  between operations  6.33 us (2%)
    pallas_call x1, Pallas kernels, fused(): pl.pallas_call(kernel, out_shape=[jax.ShapeDtypeStruct((4, 4, SLICE, TOK)...  248 us
    unnamed x25, local copies, waits for them, and re-layouts  15.7 us

profile of v1, /device:TPU:2, one launch (start us, length us, event | category | flops | bytes accessed | tf_op | source)
XLA Modules:
  0.0 296.8 jit_solution(9946493718229496730)
XLA Ops:
  0.7 1.2 dynamic_slice.86
  4.7 1.2 dynamic_slice.80
  8.8 1.2 convert_reduce_fusion.2
  10.5 1.2 convert_reduce_fusion
  11.8 1.2 convert_reduce_fusion.1
  16.3 0.9 bitcast_dynamic-update-slice_fusion.5
  17.2 0.9 bitcast_dynamic-update-slice_fusion.4
  18.1 0.9 bitcast_dynamic-update-slice_fusion.3
  19.0 0.9 bitcast_dynamic-update-slice_fusion.2
  19.9 0.9 bitcast_dynamic-update-slice_fusion.1
  20.8 0.9 bitcast_dynamic-update-slice_fusion.wown
  21.8 1.1 copy.60.cols
  24.1 1.0 fusion.1.keys
  25.1 3.0 copy.55
  29.6 4.4 %copy.56 = bf16[256,5120]{0,1:T(8,128)(2,1)} copy(bf16[256,5120]{1,0:T(8,128)(2,1)} %param.17) | data formatting | bytes 5242880 | tf_op args[1]
  33.9 1.2 constant_dynamic-slice_fusion
  36.5 1.1 fusion.7.a1
  37.5 247.9 %shard_map.167 = (bf16[4,4,320,256]{3,2,1,0:T(8,128)(2,1)}, f32[256,128]{1,0:T(8,128)}, f32[256,128]{1,0:T(8,128)}, f32[8,128]{1,0:T(8,128)}) custom-call(bf16[6,80,640]{2,1,0:T(8,128)(2,1)} %copy-done.6, bf16[1280,256]{1,0:T(8,128)(2,1)} %fusion.7.a1, bf16[320,256]{1,0:T(8,128)(2,1)} %dynamic-slice_bitcast_fusion.1.x1s, ...), custom_call_target="tpu_custom_call" | custom-call | flops 8000000000 | bytes 10000000 | tf_op jit(solution)/shard_map/pallas_call | solution.py:502
  285.5 1.3 slice_reduce_fusion.1
  287.5 2.0 copy.67
  289.7 1.2 convert_multiply_fusion.2
  290.9 1.2 fusion.19
  292.1 1.1 copy.64
  295.3 1.5 copy.65
  (61 shorter events, 11.2 us)
Async XLA Ops:
  0.6 14.1 %copy-start.7 = (s32[1,256]{1,0:T(1,128)S(1)}, s32[1,256]{1,0:T(1,128)}, u32[]{:S(2)}) copy-start(s32[1,256]{1,0:T(1,128)} %param.20) | copy-start | bytes 3076
  13.2 9.7 %copy-start.1 = (bf16[1,512,640]{2,1,0:T(8,128)(2,1)S(1)}, bf16[1,512,640]{2,1,0:T(8,128)(2,1)}, u32[]{:S(2)}) copy-start(bf16[1,512,640]{2,1,0:T(8,128)(2,1)} %param.30) | copy-start | bytes 1966084
  21.8 1.1 copy-start.6
  287.5 2.1 copy-start.4
  287.5 2.1 copy-start.5
  293.2 1.3 copy-start
  293.2 1.5 copy-start.2
  293.2 1.7 copy-start.3

commit v2 on v1

--- a/solution.py
+++ b/solution.py
@@ -17,7 +17,6 @@
 SLICE = 320
 QUARTER = 1280
 QROWS = TOK + 16
-QCOLS = COLS + 128
 LAG = 3
 EPSILON = 1e-06
 FLOOR_EPSILON = 1e-05
@@ -59,8 +58,8 @@
 YMC = SLOTS.take(4)
 YPR = SLOTS.take(4)
 YGN = SLOTS.take(4)
-YNO = SLOTS.take(4)
-YCO = SLOTS.take(4)
+YRR = SLOTS.take(4)
+YIN = SLOTS.take(4)
 YGM = SLOTS.take(4)
 YGQ = SLOTS.take(4)
 YGH = SLOTS.take(4)
@@ -74,11 +73,13 @@
 
 
 def kernel(
-    wown, a1, x1s, nzs, onehot, shifts, cols, scols, r1, keys, values,
-    out4, ss_out, inner_out, dist_out,
+    gen_steps, critic_steps, row_order, gen_input, noise,
+    w_gq, w_go, w_tq, w_to, w_fq, w_fo, tab_g, tab_t, tab_f, text_keys, text_values,
+    out_p, out_g,
     W, qsg, qsc, qbuf, qA, qq, probs, mb, PP, CC, SS, XX, G, an,
-    send_p, send_c, send_h, gms, gmb, gq, isend, irecv, dsend, drecv,
-    ssem, rsem,
+    xv, nv, tg, tt, tf, kraw, keys, values, modv, sel, xT, onehot, colsT,
+    send_p, send_f, pbuf, fbuf, cots, gms, gmb, gq, rsend, rrecv, isend, irecv, irow, dsend, drecv,
+    ssem, rsem, lsem,
 ):
     g = lax.axis_index("group")
     s = lax.axis_index("seq")
@@ -96,6 +97,8 @@
     s_far = z_far * 2 + xh
     others = [lax.rem(g + k, GROUPS) for k in (1, 2, 3)]
     pending = []
+    own_w = [w.at[pl.ds(pl.multiple_of(g * SUB, 16), SUB)] for w in (w_gq, w_go, w_tq, w_fq, w_to, w_fo)]
+    sample = s // 8
 
     def rdma(src, dst, send, recv, **where):
         return pltpu.make_async_remote_copy(
@@ -106,6 +109,17 @@
     def start(copy):
         copy.start()
         pending.append(copy)
+
+    mine_of_d = pl.ds(pl.multiple_of(m * QUARTER, 128), QUARTER)
+    loads = [
+        pltpu.make_async_copy(gen_input, xv, lsem.at[0]),
+        pltpu.make_async_copy(tab_g, tg, lsem.at[1]),
+        pltpu.make_async_copy(tab_t, tt, lsem.at[2]),
+        pltpu.make_async_copy(tab_f, tf, lsem.at[3]),
+        pltpu.make_async_copy(text_keys.at[0], kraw, lsem.at[4]),
+        pltpu.make_async_copy(text_values.at[0], values, lsem.at[5]),
+        pltpu.make_async_copy(noise.at[:, mine_of_d], nv, lsem.at[6]),
+    ]
 
     barrier = pltpu.get_barrier_semaphore()
     peers = [{"group": o} for o in others]
@@ -121,7 +135,7 @@
         sem = RING + (way * 6 + k) * 7 + t
         if way == 0:
             rows = rows_of(z - t, xh)
-            src = wown.at[k] if t == 0 else W.at[k, rows]
+            src = own_w[k] if t == 0 else W.at[k, rows]
             return rdma(src, W.at[k, rows], sem, sem, seq=s_up)
         rows = rows_of(z + t, 1 - xh)
         return rdma(W.at[k, rows], W.at[k, rows], sem, sem, seq=s_down)
@@ -133,9 +147,8 @@
 
     my_rows = rows_of(z, xh)
     for k in range(6):
-        start(rdma(wown.at[k], W.at[k, my_rows], XCH + k, XCH + k, seq=s_x))
-    for k in range(6):
-        W[k, my_rows, :] = wown[k]
+        start(rdma(own_w[k], W.at[k, my_rows], XCH + k, XCH + k, seq=s_x))
+    own_loads = [pltpu.make_async_copy(own_w[k], W.at[k, my_rows], lsem.at[7 + k]) for k in range(6)]
 
     state = {"tick": 0}
 
@@ -160,6 +173,7 @@
 
     def have(k):
         ring_to(LAG * k + 6)
+        own_loads[k].wait()
 
     def y_send(base, dg, src, dst):
         start(rdma(src, dst, base + dg, base + g, group=others[dg - 1]))
@@ -234,19 +248,60 @@
 
     def gathered(own):
         parts = [own] + [qbuf.at[o] for o in others]
-        total = sum(p[0:TOK, 0:COLS].astype(F32) for p in parts)
-        bias = sum(p[TOK:QROWS, 0:COLS].astype(F32) for p in parts)[0:1, :]
-        extra = sum(p[0:TOK, COLS:QCOLS].astype(F32) for p in parts)
-        return total, bias, extra
-
-    def to_bf_rows(ref, part, bias, extra):
-        ref[0:TOK, 0:COLS] = part.astype(BF)
-        ref[TOK:QROWS, 0:COLS] = bias.astype(BF)
-        ref[0:TOK, COLS:QCOLS] = extra
-        ref[TOK:QROWS, COLS:QCOLS] = jnp.zeros((16, 128), BF)
-
+        total = sum(p[0:TOK, :].astype(F32) for p in parts)
+        bias = sum(p[TOK:QROWS, :].astype(F32) for p in parts)[0:1, :]
+        return total, bias
+
+    def to_bf_rows(ref, part, bias):
+        ref[0:TOK, :] = part.astype(BF)
+        ref[TOK:QROWS, :] = jnp.broadcast_to(bias, (16, COLS)).astype(BF)
+
+    ring_to(0)
+    for copy in loads + own_loads:
+        copy.start()
+    row = lax.broadcasted_iota(jnp.int32, (2 * SUB, 2 * SLICE), 0)
+    col = lax.broadcasted_iota(jnp.int32, (2 * SUB, 2 * SLICE), 1)
+    base = row + jnp.where(row >= SUB, SLICE - SUB, 0)
+    for o in range(4):
+        sel[o] = (col == base + o * SUB).astype(BF)
+    order = lax.broadcasted_iota(jnp.int32, (TOK, TOK), 0)
+    onehot[...] = (order == row_order[...]).astype(BF)
+    modv[...] = jnp.zeros_like(modv)
+    for copy in loads:
+        copy.wait()
+    modv[0:3, :] = tg[gen_steps[sample]].astype(F32)
+    modv[3:6, :] = tt[critic_steps[sample]].astype(F32)
+    modv[6:9, :] = tf[critic_steps[sample]].astype(F32)
+    own_sel = sel[g]
+    square_row = jnp.zeros((8, TOK), F32)
+    square_col = jnp.zeros((TOK, 128), F32)
+    for w in range(8):
+        window = pl.ds(w * 2 * SLICE, 2 * SLICE)
+        rows = pl.ds(w * 2 * SUB, 2 * SUB)
+        part = xv[:, window]
+        xw = dot_nt(own_sel, part)
+        cw = dot_nt(own_sel, modv[:, window].astype(BF))
+        colsT[rows, :] = cw
+        xT[rows, :] = xw.astype(BF)
+        an[0, rows, :] = (xw * (1.0 + cw[:, 1:2])).astype(BF)
+        sq = part.astype(F32)
+        sq = (sq * sq).astype(BF)
+        square_row = square_row + dot_nt(jnp.ones((8, 2 * SLICE), BF), sq)
+        square_col = square_col + dot_nn(sq, jnp.ones((2 * SLICE, 128), BF))
+    r1_row = lax.rsqrt(square_row[0:1, :] * (1.0 / D) + EPSILON)
+    r1 = lax.rsqrt(square_col[:, 0:1] * (1.0 / D) + EPSILON)
+    for h in range(HEADS):
+        lanes = pl.ds(h * HEAD, HEAD)
+        kf = kraw[:, lanes].astype(F32)
+        keys[:, lanes] = (kf * lax.rsqrt(jnp.mean(kf * kf, axis=1, keepdims=True) + EPSILON)).astype(BF)
+    cols_b = colsT[...].astype(BF)
+    mine = slice_rows(m)
+    scols = colsT[mine, :]
+    gate_g, gate_t, gate_f = scols[:, 2:3], scols[:, 5:6], scols[:, 8:9]
+    angle = jnp.full((8, 128), critic_steps[sample] + 1).astype(F32) * (0.5 * 3.141592653589793 / (tg.shape[0] + 1.0))
+    alpha, sigma = jnp.cos(angle)[0:1, 0:1], jnp.sin(angle)[0:1, 0:1]
     have(GQ)
-    to_bf_rows(qsg, dot_tn(a1[...], W[GQ]), dot_nn(shifts[0], W[GQ]), jnp.zeros((TOK, 128), BF))
+    to_bf_rows(qsg, dot_tn(an[0], W[GQ]), dot_tn(cols_b, W[GQ])[0:1])
     gen_q = rdma(qsg, qbuf.at[g], YQG, YQG + g, group=0)
 
     @pl.when(g != 0)
@@ -261,8 +316,8 @@
     def _():
         for o in others:
             y_wait(YQG, o, qbuf.at[o])
-        total, bias, _ = gathered(qsg)
-        attend(r1[...], total, bias)
+        total, bias = gathered(qsg)
+        attend(r1, total, bias)
         for copy in (gen_m[1], gen_m[0], gen_m[2]):
             copy.start()
 
@@ -276,30 +331,27 @@
     rs_first(0)
     rs_second(0)
     total = rs_total(0)
-    gate_g, gate_t, gate_f = scols[:, 0:1], scols[:, 1:2], scols[:, 2:3]
-    alpha, sigma = scols[:, 3:4], scols[:, 4:5]
-    gen_s = (x1s[...].astype(F32) + gate_g * total).astype(BF)
+    gen_s = (xT[mine, :].astype(F32) + gate_g * total).astype(BF)
     send_p[0] = gen_s
     arr = dot_nn(gen_s, onehot[...])
-    noised = (alpha * arr + sigma * nzs[...].astype(F32)).astype(BF)
-    G[0, slice_rows(m), :] = noised
+    nzs = jnp.concatenate([dot_nt(own_sel, nv[:, pl.ds(w * 2 * SLICE, 2 * SLICE)]) for w in (0, 1)], axis=0)
+    noised = (alpha * arr + sigma * nzs).astype(BF)
+    G[0, mine, :] = noised
     ag_first(0)
     ag_second(0)
     ag_wait(0)
 
     nf = G[0].astype(F32)
     sq = (nf * nf).astype(BF)
-    squares = dot_tn(sq, jnp.ones((QUARTER, 128), BF))
-    high = squares.astype(BF)
-    low = (squares - high.astype(F32)).astype(BF)
-    lane = lax.broadcasted_iota(jnp.int32, (TOK, 128), 1)
-    extra = jnp.where(lane < 64, high.astype(F32), low.astype(F32)).astype(BF)
-    an[0] = (nf * cols[:, 0:1]).astype(BF)
-    an[1] = (nf * cols[:, 1:2]).astype(BF)
+    rsend[...] = dot_nn(jnp.ones((8, QUARTER), BF), sq)
+    for k in (2, 1, 3):
+        y_send(YRR, k, rsend, rrecv.at[g])
+    an[0] = (nf * (1.0 + colsT[:, 4:5])).astype(BF)
+    an[1] = (nf * (1.0 + colsT[:, 7:8])).astype(BF)
     have(TQ)
-    to_bf_rows(qsc.at[0], dot_tn(an[0], W[TQ]), dot_nn(shifts[1], W[TQ]), extra)
+    to_bf_rows(qsc.at[0], dot_tn(an[0], W[TQ]), dot_tn(cols_b, W[TQ])[3:4])
     have(FQ)
-    to_bf_rows(qsc.at[1], dot_tn(an[1], W[FQ]), dot_nn(shifts[2], W[FQ]), extra)
+    to_bf_rows(qsc.at[1], dot_tn(an[1], W[FQ]), dot_tn(cols_b, W[FQ])[6:7])
     crit_q = []
     for k in (2, 1, 3):
         t = others[k - 1]
@@ -310,23 +362,21 @@
             copy.start()
 
     have(TO)
+    square_row = rsend[...]
+    for o in others:
+        y_wait(YRR, o, rrecv.at[o])
+        square_row = square_row + rrecv[o]
+    rn_row = lax.rsqrt(square_row[0:1, :] * (1.0 / D) + EPSILON)
     crit_m = [rdma(mb.at[g], mb.at[g], YMC + k, YMC + g, group=others[k - 1]) for k in (1, 2, 3)]
 
     @pl.when(g != 0)
     def _():
         for o in others:
             y_wait(YQC, o, qbuf.at[o])
-        total, bias, extra = gathered(qsc.at[g // 3])
-        square = extra[:, 0:1] + extra[:, 64:65]
-        r = lax.rsqrt(square * (1.0 / D) + EPSILON)
-        ss_out[...] = jnp.broadcast_to(r, (TOK, 128))
-        attend(r, total, bias)
+        total, bias = gathered(qsc.at[g // 3])
+        attend(jnp.transpose(jnp.broadcast_to(rn_row, (128, TOK)))[:, 0:1], total, bias)
         for copy in (crit_m[1], crit_m[0], crit_m[2]):
             copy.start()
-
-    @pl.when(g == 0)
-    def _():
-        ss_out[...] = jnp.broadcast_to(r1[...], (TOK, 128))
 
     have(FO)
     for r in (1, 2, 3):
@@ -335,9 +385,7 @@
             y_wait(YMC, r, mb.at[r])
         planes(r, TO if r < 3 else FO, mb.at[r])
         rs_first(r)
-    for k in (2, 1, 3):
-        y_send(YNO, k, G.at[0, slice_rows(m)], out4.at[2, g])
-    gen_p = rdma(send_p.at[0], out4.at[0, g], YGN, YGN + g, group=0)
+    gen_p = rdma(send_p.at[0], pbuf.at[g], YGN, YGN + g, group=0)
 
     @pl.when(g != 0)
     def _():
@@ -352,19 +400,17 @@
     crit_p = []
     for k in (2, 1, 3):
         t = others[k - 1]
-        crit_p.append((t, rdma(send_p.at[t], out4.at[0, g], YPR + k, YPR + g, group=t)))
+        crit_p.append((t, rdma(send_p.at[t], pbuf.at[g], YPR + k, YPR + g, group=t)))
 
     cond, uncond, faked = [send_p[r].astype(F32) for r in (1, 2, 3)]
     real = GUIDANCE * cond - (GUIDANCE - 1.0) * uncond
     score = faked - real
     score_b = score.astype(BF)
     gen_cot = dot_nt(score_b, onehot[...])
-    send_c[0] = gen_cot.astype(BF)
-    send_c[1] = score_b
-    send_c[2] = score_b
     fake_cot = faked - arr
-    send_c[3] = fake_cot.astype(BF)
-    mine = slice_rows(m)
+    cots[0] = gen_cot
+    cots[1] = score
+    cots[2] = fake_cot
     G[1, mine, :] = (gate_g * gen_cot).astype(BF)
     ag_first(1)
     G[2, mine, :] = (gate_t * score).astype(BF)
@@ -423,7 +469,7 @@
     inner = lax.fori_loop(0, HEADS, head_back, jnp.zeros((TOK, 1), F32))
     for k in (2, 1, 3):
         y_send(YGQ, k, gq.at[g], gq.at[g])
-    isend[0] = jnp.broadcast_to(inner, (TOK, 128))
+    isend[0] = jnp.transpose(jnp.broadcast_to(inner, (TOK, 128)))[0:8, :]
     start(rdma(isend.at[0], irecv.at[0], INN, INN, mp=m_core))
     butterfly_end(1)
     start(butterfly(2))
@@ -432,6 +478,10 @@
     start(rdma(isend.at[1], irecv.at[1], INN + 1, INN + 1, mp=m_x))
     butterfly_end(2)
     start(butterfly(3))
+    rdma(irecv.at[1], irecv.at[1], INN + 1, INN + 1, mp=m_x).wait_recv()
+    irow[g] = isend[1] + irecv[1]
+    for k in (2, 1, 3):
+        y_send(YIN, k, irow.at[g], irow.at[g])
 
     for r in range(4):
         @pl.when(g != r)
@@ -443,50 +493,56 @@
     start(butterfly(4))
     for r in range(4):
         rs_second(4 + r)
-    for k in (2, 1, 3):
-        t = others[k - 1]
-        y_send(YCO, k, send_c.at[t], out4.at[1, g])
-    for r in range(4):
-        send_h[r] = rs_total(4 + r).astype(BF)
-    for k in (2, 1, 3):
-        t = others[k - 1]
-        y_send(YGH, k, send_h.at[t], out4.at[3, g])
     butterfly_end(4)
     for k in (2, 1, 3):
         y_send(YDI, k, dsend.at[5], drecv.at[5 + g])
-    rdma(irecv.at[1], irecv.at[1], INN + 1, INN + 1, mp=m_x).wait_recv()
-    inner_out[...] = isend[1] + irecv[1]
-    out4[0, g] = send_p[g]
-    out4[1, g] = send_c[g]
-    out4[2, g] = G[0, mine, :]
-    out4[3, g] = send_h[g]
     total = dsend[5]
     for o in others:
         y_wait(YDI, o, drecv.at[5 + o])
         total = total + drecv[5 + o]
-    dist_out[...] = total
-
+    count = float(TOK * 16 // SAMPLES * D)
+    inverse = 1.0 / (jnp.sum(total[0:1, :], axis=1, keepdims=True) * (1.0 / count) + FLOOR_EPSILON)
     for o in others:
-        y_wait(YNO, o, out4.at[2, o])
-        y_wait(YCO, o, out4.at[1, o])
-        y_wait(YGH, o, out4.at[3, o])
+        y_wait(YIN, o, irow.at[o])
+    for r in range(4):
+        scale = 1.0 + scols[:, (1, 4, 4, 7)[r]:(1, 4, 4, 7)[r] + 1]
+        rr = r1_row if r == 0 else rn_row
+        rows = xT[mine, :].astype(F32) if r == 0 else own_n
+        ct = (1.0, -GUIDANCE, GUIDANCE - 1.0, 1.0)[r] * cots[(0, 1, 1, 2)[r]]
+        grads = ct + rr * scale * rs_total(4 + r) - rows * (rr * rr * rr * (irow[r][0:1, :] * (1.0 / D)))
+        send_f[r] = (grads if r == 3 else grads * inverse).astype(BF)
+    for k in (2, 1, 3):
+        y_send(YGH, k, send_f.at[others[k - 1]], fbuf.at[g])
+    pbuf[g] = send_p[g]
+    fbuf[g] = send_f[g]
+
+    def assemble(buf, w):
+        rows = pl.ds(w * 2 * SUB, 2 * SUB)
+        return sum(dot_tn(buf[o, rows, :], sel[o]) for o in range(4))
 
     @pl.when(g == 0)
     def _():
         for o in others:
-            y_wait(YGN, o, out4.at[0, o])
+            y_wait(YGN, o, pbuf.at[o])
         for copy in gen_m:
             copy.wait_send()
 
     @pl.when(g != 0)
     def _():
         for o in others:
-            y_wait(YPR, o, out4.at[0, o])
+            y_wait(YPR, o, pbuf.at[o])
         gen_q.wait_send()
         gen_p.wait_send()
         for copy in crit_m:
             copy.wait_send()
 
+    for w in (0, 1):
+        out_p[0, :, pl.ds(w * 2 * SLICE, 2 * SLICE)] = assemble(pbuf, w).astype(BF)
+    for o in others:
+        y_wait(YGH, o, fbuf.at[o])
+    for w in (0, 1):
+        out_g[0, :, pl.ds(w * 2 * SLICE, 2 * SLICE)] = assemble(fbuf, w)
+
     for t, copy in crit_q + crit_p:
         @pl.when(t != 0)
         def _():
@@ -496,24 +552,26 @@
         copy.wait_send()
 
 
-def fused(*operands):
+def on_device(*operands):
     vmem = pl.BlockSpec(memory_space=pltpu.VMEM)
+    smem = pl.BlockSpec(memory_space=pltpu.SMEM)
+    hbm = pl.BlockSpec(memory_space=pl.ANY)
     act = lambda *lead: pltpu.VMEM(lead + (SLICE, TOK), BF)
+    (gen_input, noise, gen_steps, critic_steps, row_order) = operands[:5]
+    table = pltpu.VMEM(operands[11].shape, BF)
     return pl.pallas_call(
         kernel,
         out_shape=[
-            jax.ShapeDtypeStruct((4, 4, SLICE, TOK), BF),
-            jax.ShapeDtypeStruct((TOK, 128), F32),
-            jax.ShapeDtypeStruct((TOK, 128), F32),
-            jax.ShapeDtypeStruct((8, 128), F32),
+            jax.ShapeDtypeStruct((1, TOK, QUARTER), BF),
+            jax.ShapeDtypeStruct((1, TOK, QUARTER), F32),
         ],
-        in_specs=[vmem] * len(operands),
-        out_specs=[vmem] * 4,
+        in_specs=[smem, smem, vmem] + [hbm] * 13,
+        out_specs=[vmem] * 2,
         scratch_shapes=[
             pltpu.VMEM((6, QUARTER, COLS), BF),
-            pltpu.VMEM((QROWS, QCOLS), BF),
-            pltpu.VMEM((2, QROWS, QCOLS), BF),
-            pltpu.VMEM((4, QROWS, QCOLS), BF),
+            pltpu.VMEM((QROWS, COLS), BF),
+            pltpu.VMEM((2, QROWS, COLS), BF),
+            pltpu.VMEM((4, QROWS, COLS), BF),
             pltpu.VMEM((TOK, COLS), F32),
             pltpu.VMEM((TOK, COLS), F32),
             pltpu.VMEM((HEADS, TOK, TEXT), BF),
@@ -524,101 +582,43 @@
             act(8),
             pltpu.VMEM((4, QUARTER, TOK), BF),
             pltpu.VMEM((2, QUARTER, TOK), BF),
+            pltpu.VMEM((TOK, D), BF),
+            pltpu.VMEM((TOK, QUARTER), BF),
+            table,
+            table,
+            table,
+            pltpu.VMEM((TEXT, COLS), BF),
+            pltpu.VMEM((TEXT, COLS), BF),
+            pltpu.VMEM((TEXT, COLS), BF),
+            pltpu.VMEM((16, D), F32),
+            pltpu.VMEM((4, 2 * SUB, 2 * SLICE), BF),
+            pltpu.VMEM((QUARTER, TOK), BF),
+            pltpu.VMEM((TOK, TOK), BF),
+            pltpu.VMEM((QUARTER, 16), F32),
             act(4),
             act(4),
             act(4),
+            act(4),
+            pltpu.VMEM((3, SLICE, TOK), F32),
             pltpu.VMEM((3, TOK, COLS), BF),
             pltpu.VMEM((4, TOK, COLS), BF),
             pltpu.VMEM((4, TOK, COLS), BF),
-            pltpu.VMEM((2, TOK, 128), F32),
-            pltpu.VMEM((2, TOK, 128), F32),
+            pltpu.VMEM((8, TOK), F32),
+            pltpu.VMEM((4, 8, TOK), F32),
+            pltpu.VMEM((2, 8, TOK), F32),
+            pltpu.VMEM((2, 8, TOK), F32),
+            pltpu.VMEM((4, 8, TOK), F32),
             pltpu.VMEM((6, 8, 128), F32),
             pltpu.VMEM((9, 8, 128), F32),
             pltpu.SemaphoreType.DMA((N_SEM,)),
             pltpu.SemaphoreType.DMA((N_SEM,)),
+            pltpu.SemaphoreType.DMA((13,)),
         ],
         compiler_params=pltpu.CompilerParams(
             collective_id=0, has_side_effects=True, vmem_limit_bytes=60 * 2**20
         ),
         cost_estimate=pl.CostEstimate(flops=8 * 10**9, bytes_accessed=10**7, transcendentals=10**6),
-    )(*operands)
-
-
-def on_device(
-    gen_input, noise, gen_steps, critic_steps, row_order,
-    gen_wq, gen_wo, teacher_wq, teacher_wo, fake_wq, fake_wo,
-    gen_mod, teacher_mod, fake_mod, text_keys, text_values,
-):
-    g = lax.axis_index("group")
-    s = lax.axis_index("seq")
-    m = lax.axis_index("mp")
-    sample = s // (lax.axis_size("seq") // SAMPLES)
-    is_gen = g == 0
-    is_fake = g == GROUPS - 1
-    step_count = gen_mod.shape[0]
-
-    def pick(values, index, axis):
-        return lax.dynamic_index_in_dim(values, index, axis, keepdims=False)
-
-    def quarter(values):
-        return pick(values.reshape(values.shape[:-1] + (16, 4, SUB)), g, values.ndim).reshape(
-            values.shape[:-1] + (QUARTER,)
-        )
-
-    def own_slice(values):
-        return lax.dynamic_slice_in_dim(values, m * SLICE, SLICE, values.ndim - 1)
-
-    def block(values):
-        return lax.dynamic_slice_in_dim(values, m * QUARTER, QUARTER, values.ndim - 1)
-
-    gen_step = pick(gen_steps, sample, 0)
-    critic_step = pick(critic_steps, sample, 0)
-    mod_g = pick(gen_mod, gen_step, 0).astype(F32)
-    mod_t = pick(teacher_mod, critic_step, 0).astype(F32)
-    mod_f = pick(fake_mod, critic_step, 0).astype(F32)
-    quarter_g, quarter_t, quarter_f = quarter(mod_g), quarter(mod_t), quarter(mod_f)
-
-    x = gen_input.astype(F32)
-    r1 = lax.rsqrt(jnp.mean(x * x, axis=1, keepdims=True) + EPSILON)
-    xq = quarter(gen_input)
-    a1 = (xq.astype(F32) * (1.0 + quarter_g[1])).astype(BF).T
-    x1s = own_slice(xq).T
-    nzs = own_slice(quarter(noise)).T
-    order = row_order[0]
-    onehot = (jnp.arange(TOK, dtype=jnp.int32)[:, None] == order[None, :]).astype(BF)
-    shifts = jnp.broadcast_to(
-        jnp.stack([quarter_g[0], quarter_t[0], quarter_f[0]])[:, None, :], (3, 16, QUARTER)
-    ).astype(BF)
-    angle = 0.5 * jnp.pi * (critic_step.astype(F32) + 1.0) / (step_count + 1.0)
-    cols = jnp.stack([1.0 + quarter_t[1], 1.0 + quarter_f[1]], axis=1)
-    ones = jnp.ones((SLICE,), F32)
-    scols = jnp.stack(
-        [own_slice(quarter_g[2]), own_slice(quarter_t[2]), own_slice(quarter_f[2]),
-         ones * jnp.cos(angle), ones * jnp.sin(angle)], axis=1)
-    wown = jnp.stack([
-        lax.dynamic_slice_in_dim(w, g * SUB, SUB, 0)
-        for w in (gen_wq, gen_wo, teacher_wq, fake_wq, teacher_wo, fake_wo)
-    ])
-    kf = text_keys[0].astype(F32).reshape(TEXT, HEADS, HEAD)
-    keys = (kf * lax.rsqrt(jnp.mean(kf * kf, axis=2, keepdims=True) + EPSILON)).astype(BF)
-    keys = keys.reshape(TEXT, COLS)
-
-    out4, r_cols, inner_cols, dist = fused(
-        wown, a1, x1s, nzs, onehot, shifts, cols, scols, r1, keys, text_values[0]
-    )
-    rows = out4.reshape(4, 4, 4, SUB, TOK).transpose(0, 4, 2, 1, 3).reshape(4, TOK, QUARTER)
-    predictions = rows[0]
-    cot, noised, grad_hidden = rows[1].astype(F32), rows[2].astype(F32), rows[3].astype(F32)
-    r = r_cols[:, 0:1]
-    inner = inner_cols[:, 0:1] * (1.0 / D)
-    sample_size = float(TOK * lax.axis_size("seq") // SAMPLES * D)
-    denominator = jnp.sum(dist[0]) / sample_size + FLOOR_EPSILON
-    scale = block(jnp.where(is_gen, mod_g[1], jnp.where(is_fake, mod_f[1], mod_t[1])))
-    x_rows = jnp.where(is_gen, block(x), noised)
-    factor = jnp.where(g == 1, -GUIDANCE, jnp.where(g == 2, GUIDANCE - 1.0, 1.0))
-    grads = factor * cot + r * (1.0 + scale) * grad_hidden - x_rows * (r * r * r * inner)
-    grads = grads * jnp.where(is_fake, 1.0, 1.0 / denominator)
-    return (predictions[None], grads[None])
+    )(gen_steps, critic_steps, row_order, gen_input, noise, *operands[5:])
 
 
 def solution(mesh):

time: 298 us -> 256 us (0.86)
  local copies, waits for them, and re-layouts: 30.8 us -> 10.4 us
  other arithmetic: 11.8 us -> 0 us
  between operations: 6.33 us -> 0.65 us
  Pallas kernels: 248 us -> 245 us
    convert_element_type x6 -> x0, other arithmetic: 5.52 us -> none  [the longest x1 1.16 us: on_device(): mod_g = pick(gen_mod, gen_step, 0).astype(F32)]
    unnamed x25 -> x7, local copies, waits for them, and re-layouts: 15.7 us -> 10.4 us
    dynamic_slice x6 -> x0, local copies, waits for them, and re-layouts: 3.89 us -> none  [the longest x3 3.66 us: pick(): return lax.dynamic_index_in_dim(values, index, axis, keepdims=False)]
    pallas_call x1, Pallas kernels: 248 us -> 245 us  [on_device(): pl.pallas_call(kernel, out_shape=[jax.ShapeDtypeStruct((1, TOK, QUARTER),...]
where the time goes in v2:
time: 256 us
  Pallas kernels  245 us (96%)
  local copies, waits for them, and re-layouts  10.4 us (4%)
    pallas_call x1, Pallas kernels, on_device(): pl.pallas_call(kernel, out_shape=[jax.ShapeDtypeStruct((1, TOK, QUARTER),...  245 us
    unnamed x7, local copies, waits for them, and re-layouts  10.4 us

profile of v2, /device:TPU:2, one launch (start us, length us, event | category | flops | bytes accessed | tf_op | source)
XLA Modules:
  0.0 255.7 jit_solution(17369443465282412066)
XLA Ops:
  0.6 0.0 copy-start
  0.6 2.3 copy.18.tab_g
  3.0 2.3 copy.19.tab_t
  5.3 0.0 copy-done
  5.3 1.3 copy.20.tab_f
  6.6 244.7 %shard_map.167 = (bf16[1,256,1280]{2,1,0:T(8,128)(2,1)}, f32[1,256,1280]{2,1,0:T(8,128)}) custom-call(s32[2]{0:T(128)} %gen_steps.1, s32[2]{0:T(128)} %critic_steps.1, s32[1,256]{1,0:T(1,128)} %row_order.1, bf16[256,5120]{1,0:T(8,128)(2,1)} %gen_input.1, bf16[256,5120]{1,0:T(8,128)(2,1)} %noise.1, bf16[320,640]{1,0:T(8,128)(2,1)} %w_gq.1, ...), custom_call_target="tpu_custom_call" | custom-call | flops 8000000000 | bytes 10000000 | tf_op jit(solution)/shard_map/pallas_call | solution.py:562
  251.3 2.0 copy.23
  253.3 2.5 copy.24
Async XLA Ops:
  0.6 4.6 %copy-start = (bf16[16,3,5120]{2,0,1:T(8,128)(2,1)S(1)}, bf16[16,3,5120]{2,0,1:T(8,128)(2,1)}, u32[]{:S(2)}) copy-start(bf16[16,3,5120]{2,0,1:T(8,128)(2,1)} %param.29) | copy-start | bytes 1474564

commit v3 on v2

v3 whole, which is shorter than its diff:
```python
import jax
import jax.numpy as jnp
from jax import lax
from jax.experimental import pallas as pl
from jax.experimental.pallas import tpu as pltpu
from jax.sharding import PartitionSpec as P

D = 5120
HEAD = 128
SAMPLES = 2
GROUPS = 4
TOK = 256
TEXT = 512
COLS = 640
HEADS = 5
SUB = 80
SLICE = 320
QUARTER = 1280
QROWS = TOK + 16
HALF = 128
RING_START = (0, 2, 4, 6, 8, 10)
X_LAST = (False, True, False, True, False, True)
EPSILON = 1e-06
FLOOR_EPSILON = 1e-05
GUIDANCE = 3.0
BF = jnp.bfloat16
F32 = jnp.float32

GQ, GO, TQ, FQ, TO, FO = range(6)


def dot_nn(a, b):
    return lax.dot_general(a, b, (((1,), (0,)), ((), ())), preferred_element_type=F32)


def dot_nt(a, b):
    return lax.dot_general(a, b, (((1,), (1,)), ((), ())), preferred_element_type=F32)


def dot_tn(a, b):
    return lax.dot_general(a, b, (((0,), (0,)), ((), ())), preferred_element_type=F32)


class Slots:
    def __init__(self):
        self.count = 0

    def take(self, number):
        first = self.count
        self.count += number
        return first


SLOTS = Slots()
RING = SLOTS.take(6 * 16)
XCH = SLOTS.take(6 * 8)
YQG = SLOTS.take(8)
YQC = SLOTS.take(8)
YMG = SLOTS.take(8)
YMC = SLOTS.take(8)
YGM = SLOTS.take(8)
YGQ = SLOTS.take(8)
YGH = SLOTS.take(8)
YRR = SLOTS.take(8)
YPR = SLOTS.take(4)
YGN = SLOTS.take(4)
YIN = SLOTS.take(4)
YDI = SLOTS.take(4)
RSC = SLOTS.take(8 * 2 * 2)
RSX = SLOTS.take(8 * 2)
AGM = SLOTS.take(4 * 2 * 3)
BUT = SLOTS.take(5)
INN = SLOTS.take(2)
N_SEM = SLOTS.count


def kernel(
    gen_steps, critic_steps, row_order, gen_input, noise,
    w_gq, w_go, w_tq, w_to, w_fq, w_fo, tab_g, tab_t, tab_f, text_keys, text_values,
    out_p, out_g,
    W, qsg, qsc, qbuf, qA, qq, probs, mb, PP, CC, SS, XX, G, an,
    xv, nv, tg, tt, tf, kraw, keys, values, modv, sel, xT, onehot, colsT,
    send_p, send_f, pbuf, fbuf, cots, gms, gmb, gq, rsend, rrecv, isend, irecv, irow, dsend, drecv,
    ssem, rsem, lsem,
):
    g = lax.axis_index("group")
    s = lax.axis_index("seq")
    m = lax.axis_index("mp")
    z, xh = s // 2, lax.rem(s, 2)
    xl, c = m // 2, lax.rem(m, 2)
    m_core = 2 * xl + 1 - c
    m_x = 2 * (1 - xl) + c
    s_x = 2 * z + 1 - xh
    z_pair = z + 1 - 2 * lax.rem(z, 2)
    z_far = z + 2 - 4 * lax.rem(z // 2, 2)
    s_up = lax.rem(z + 1, 8) * 2 + xh
    s_down = lax.rem(z + 7, 8) * 2 + xh
    s_pair = z_pair * 2 + xh
    s_far = z_far * 2 + xh
    others = [lax.rem(g + k, GROUPS) for k in (1, 2, 3)]
    pending = []
    own_w = [w.at[pl.ds(pl.multiple_of(g * SUB, 16), SUB)] for w in (w_gq, w_go, w_tq, w_fq, w_to, w_fo)]
    sample = s // 8

    def rdma(src, dst, send, recv, **where):
        return pltpu.make_async_remote_copy(
            src_ref=src, dst_ref=dst, send_sem=ssem.at[send], recv_sem=rsem.at[recv],
            device_id=where, device_id_type=pl.DeviceIdType.MESH,
        )

    def start(copy):
        copy.start()
        pending.append(copy)

    mine_of_d = pl.ds(pl.multiple_of(m * QUARTER, 128), QUARTER)
    loads = [
        pltpu.make_async_copy(gen_input, xv, lsem.at[0]),
        pltpu.make_async_copy(tab_g, tg, lsem.at[1]),
        pltpu.make_async_copy(tab_t, tt, lsem.at[2]),
        pltpu.make_async_copy(tab_f, tf, lsem.at[3]),
        pltpu.make_async_copy(text_keys.at[0], kraw, lsem.at[4]),
        pltpu.make_async_copy(text_values.at[0], values, lsem.at[5]),
        pltpu.make_async_copy(noise.at[:, mine_of_d], nv, lsem.at[6]),
    ]

    barrier = pltpu.get_barrier_semaphore()
    peers = [{"group": o} for o in others]
    peers += [{"mp": m_core}, {"mp": m_x}, {"seq": s_x}, {"seq": s_up}, {"seq": s_down}, {"seq": s_far}]
    for peer in peers:
        pl.semaphore_signal(barrier, inc=1, device_id=peer, device_id_type=pl.DeviceIdType.MESH)
    pl.semaphore_wait(barrier, len(peers))

    def rows_of(zz, x):
        return pl.ds(pl.multiple_of((lax.rem(zz + 16, 8) * 2 + x) * SUB, 16), SUB)

    def steps_of(way, side):
        return 4 if way == side else 3

    def flows(k):
        return [(way, side) for side in ((0,) if X_LAST[k] else (0, 1)) for way in (0, 1)]

    def ring_sem(k, way, side, t):
        return RING + k * 16 + (way * 2 + side) * 4 + t

    def side_x(side):
        return xh if side == 0 else 1 - xh

    def ring_send(k, way, side, t):
        rows = rows_of(z - t if way == 0 else z + t, side_x(side))
        src = own_w[k] if t == 0 and side == 0 else W.at[k, rows]
        sem = ring_sem(k, way, side, t)
        start(rdma(src, W.at[k, rows], sem, sem, seq=s_up if way == 0 else s_down))

    def ring_wait(k, way, side, t):
        rows = rows_of(z - 1 - t if way == 0 else z + 1 + t, side_x(side))
        sem = ring_sem(k, way, side, t)
        rdma(W.at[k, rows], W.at[k, rows], sem, sem, seq=s_up).wait_recv()
        return rows

    def x_send(k, number, src, rows):
        start(rdma(src, W.at[k, rows], XCH + 8 * k + number, XCH + 8 * k + number, seq=s_x))

    def x_wait(k, number, zz):
        rows = rows_of(zz, 1 - xh)
        sem = XCH + 8 * k + number
        rdma(W.at[k, rows], W.at[k, rows], sem, sem, seq=s_x).wait_recv()

    my_rows = rows_of(z, xh)
    own_loads = [pltpu.make_async_copy(own_w[k], W.at[k, my_rows], lsem.at[7 + k]) for k in range(6)]
    for k in range(6):
        if not X_LAST[k]:
            x_send(k, 0, own_w[k], my_rows)

    state = {"tick": 0, "begun": 0}

    def ring_begin(tick):
        while state["begun"] < 6 and RING_START[state["begun"]] <= tick:
            k = state["begun"]
            for way in (0, 1):
                ring_send(k, way, 0, 0)
            if X_LAST[k]:
                x_send(k, 0, own_w[k], my_rows)
            else:
                x_wait(k, 0, z)
                for way in (0, 1):
                    ring_send(k, way, 1, 0)
            state["begun"] += 1

    def ring_to(last):
        while state["tick"] <= last:
            tick = state["tick"]
            ring_begin(tick)
            for k in range(6):
                t = tick - RING_START[k]
                for way, side in flows(k):
                    if 0 <= t < steps_of(way, side):
                        rows = ring_wait(k, way, side, t)
                        if t + 1 < steps_of(way, side):
                            ring_send(k, way, side, t + 1)
                        if X_LAST[k]:
                            x_send(k, 1 + 4 * way + t, W.at[k, rows], rows)
            state["tick"] += 1

    def have(k):
        ring_to(RING_START[k] + 3)
        own_loads[k].wait()
        if X_LAST[k]:
            x_wait(k, 0, z)
            for t in range(4):
                x_wait(k, 1 + t, z - 1 - t)
            for t in range(3):
                x_wait(k, 5 + t, z + 1 + t)

    def y_send(base, dg, src, dst, h=0):
        start(rdma(src, dst, base + 4 * h + dg, base + 4 * h + g, group=others[dg - 1]))

    def y_wait(base, source, ref, h=0):
        rdma(ref, ref, base, base + 4 * h + source, group=others[0]).wait_recv()

    def start_if(cond, copy):
        @pl.when(cond)
        def _():
            copy.start()
        guarded.append((cond, copy))

    guarded = []

    def part(h):
        return pl.ds(h * HALF, HALF)

    def q_message(ref, h):
        return ref.at[pl.ds(0, 16 + HALF)] if h == 0 else ref.at[pl.ds(16 + HALF, HALF)]

    def slice_rows(index):
        return pl.ds(pl.multiple_of(index * SLICE, 16), SLICE)

    def rs_first(r, h):
        base = RSC + 4 * r + 2 * h
        for far in (1, 0):
            x = 1 - xl if far else xl
            start(rdma(PP.at[r, h, slice_rows(2 * x + 1 - c)], CC.at[r, h, x], base + far, base + x, mp=m_core))

    def rs_core_wait(r, h, x):
        base = RSC + 4 * r + 2 * h
        rdma(CC.at[r, h, x], CC.at[r, h, x], base, base + x, mp=m_core).wait_recv()

    def rs_second(r, h):
        rs_core_wait(r, h, 1 - xl)
        far = PP[r, h, slice_rows(2 * (1 - xl) + c), :].astype(F32)
        SS[r, h] = (far + CC[r, h, 1 - xl].astype(F32)).astype(BF)
        start(rdma(SS.at[r, h], XX.at[r, h], RSX + 2 * r + h, RSX + 2 * r + h, mp=m_x))

    def rs_total(r, h):
        rs_core_wait(r, h, xl)
        rdma(XX.at[r, h], XX.at[r, h], RSX + 2 * r + h, RSX + 2 * r + h, mp=m_x).wait_recv()
        return (PP[r, h, slice_rows(m), :].astype(F32) + CC[r, h, xl].astype(F32)) + XX[r, h].astype(F32)

    def ag_copy(r, h, extra, index, where):
        rows = slice_rows(index)
        sem = AGM + 6 * r + 3 * h + extra
        return rdma(G.at[r, h, rows], G.at[r, h, rows], sem, sem, mp=where)

    def ag_first(r, h):
        start(ag_copy(r, h, 0, m, m_x))
        start(ag_copy(r, h, 1, m, m_core))

    def ag_second(r, h):
        ag_copy(r, h, 0, m_x, m_x).wait_recv()
        start(ag_copy(r, h, 2, m_x, m_core))

    def ag_wait(r, h):
        ag_copy(r, h, 1, m_core, m_core).wait_recv()
        ag_copy(r, h, 2, 2 * (1 - xl) + 1 - c, m_core).wait_recv()

    def planes(r, k, ref, h):
        for i in range(4):
            rows = pl.ds(i * SLICE, SLICE)
            PP[r, h, rows, :] = dot_nt(W[k, rows, :], ref[part(h), :]).astype(BF)

    scaling = HEAD ** -0.5

    def attend(r, own, h):
        tokens = part(h)
        rows = pl.ds(16 + h * HALF, HALF)
        parts = [own] + [qbuf.at[o] for o in others]
        total = sum(p[rows, :].astype(F32) for p in parts)
        bias = sum(p[0:16, :].astype(F32) for p in parts)[0:1, :]
        qA[tokens, :] = total
        qq[tokens, :] = r * total + bias
        for n in range(HEADS):
            lanes = pl.ds(n * HEAD, HEAD)
            qh = qq[tokens, lanes]
            rq = lax.rsqrt(jnp.mean(qh * qh, axis=1, keepdims=True) + EPSILON)
            e = jnp.exp(dot_nt((qh * rq).astype(BF), keys[:, lanes]) * scaling)
            p = (e * (1.0 / jnp.sum(e, axis=1, keepdims=True))).astype(BF)
            probs[n, tokens, :] = p
            mb[g, tokens, lanes] = dot_nn(p, values[:, lanes]).astype(BF)

    def to_bf_rows(ref, value, bias, h):
        ref[pl.ds(16 + h * HALF, HALF), :] = value.astype(BF)
        if h == 0:
            ref[0:16, :] = jnp.broadcast_to(bias, (16, COLS)).astype(BF)

    ring_begin(0)
    for copy in loads + own_loads:
        copy.start()
    row = lax.broadcasted_iota(jnp.int32, (2 * SUB, 2 * SLICE), 0)
    col = lax.broadcasted_iota(jnp.int32, (2 * SUB, 2 * SLICE), 1)
    base = row + jnp.where(row >= SUB, SLICE - SUB, 0)
    for o in range(4):
        sel[o] = (col == base + o * SUB).astype(BF)
    ring_to(0)
    order = lax.broadcasted_iota(jnp.int32, (TOK, TOK), 0)
    onehot[...] = (order == row_order[...]).astype(BF)
    for copy in loads:
        copy.wait()
    picked = []
    pr = lax.broadcasted_iota(jnp.int32, (16, 16), 0)
    pc = lax.broadcasted_iota(jnp.int32, (16, 16), 1)
    for n, (tab, step) in enumerate(((tg, gen_steps), (tt, critic_steps), (tf, critic_steps))):
        for j in range(3):
            hit = jnp.where(pr == 3 * n + j, (pc == step[sample]).astype(F32), 0.0).astype(BF)
            picked.append(dot_nn(hit, tab[j]))
    modv[...] = sum(picked).astype(BF)
    ring_to(1)
    own_sel = sel[g]
    square_row = jnp.zeros((8, TOK), F32)
    square_col = jnp.zeros((TOK, 128), F32)
    for w in range(8):
        window = pl.ds(w * 2 * SLICE, 2 * SLICE)
        rows = pl.ds(w * 2 * SUB, 2 * SUB)
        piece = xv[:, window]
        xw = dot_nt(own_sel, piece)
        cw = dot_nt(own_sel, modv[:, window])
        colsT[rows, :] = cw
        xT[rows, :] = xw.astype(BF)
        axw = (xw * (1.0 + cw[:, 1:2])).astype(BF)
        for h in (0, 1):
            an[0, h, rows, :] = axw[:, h * HALF:(h + 1) * HALF]
        sq = piece.astype(F32)
        sq = (sq * sq).astype(BF)
        square_row = square_row + dot_nt(jnp.ones((8, 2 * SLICE), BF), sq)
        square_col = square_col + dot_nn(sq, jnp.ones((2 * SLICE, 128), BF))
        if w == 3:
            ring_to(2)
    r1_row = lax.rsqrt(square_row[0:1, :] * (1.0 / D) + EPSILON)
    r1 = lax.rsqrt(square_col[:, 0:1] * (1.0 / D) + EPSILON)
    for n in range(HEADS):
        lanes = pl.ds(n * HEAD, HEAD)
        kf = kraw[:, lanes].astype(F32)
        keys[:, lanes] = (kf * lax.rsqrt(jnp.mean(kf * kf, axis=1, keepdims=True) + EPSILON)).astype(BF)
    cols_b = colsT[...].astype(BF)
    mine = slice_rows(m)
    scols = colsT[mine, :]
    gate_g, gate_t, gate_f = scols[:, 2:3], scols[:, 5:6], scols[:, 8:9]
    angle = jnp.full((8, 128), critic_steps[sample] + 1).astype(F32) * (0.5 * 3.141592653589793 / (tg.shape[1] + 1.0))
    alpha, sigma = jnp.cos(angle)[0:1, 0:1], jnp.sin(angle)[0:1, 0:1]

    have(GQ)
    bias = dot_tn(cols_b, W[GQ])[0:1]
    for h in (0, 1):
        to_bf_rows(qsg, dot_tn(an[0, h], W[GQ]), bias, h)
        start_if(g != 0, rdma(q_message(qsg, h), q_message(qbuf.at[g], h), YQG + 4 * h, YQG + 4 * h + g, group=0))
    ring_to(RING_START[GO] + 3)

    gen_m = []
    for h in (0, 1):
        for k in (2, 1, 3):
            gen_m.append(rdma(mb.at[0, part(h)], mb.at[0, part(h)], YMG + 4 * h + k, YMG + 4 * h, group=others[k - 1]))

    @pl.when(g == 0)
    def _():
        for h in (0, 1):
            for o in others:
                y_wait(YQG, o, q_message(qbuf.at[o], h), h)
            attend(r1[h * HALF:(h + 1) * HALF], qsg, h)
            for copy in gen_m[3 * h:3 * h + 3]:
                copy.start()

    guarded.extend((g == 0, copy) for copy in gen_m)
    have(GO)
    ring_to(RING_START[TQ] + 3)
    for h in (0, 1):
        @pl.when(g != 0)
        def _():
            y_wait(YMG, 0, mb.at[0, part(h)], h)
        planes(0, GO, mb.at[0], h)
        rs_first(0, h)
    for h in (0, 1):
        rs_second(0, h)
    ring_to(RING_START[FQ] + 3)
    for h in (0, 1):
        total = rs_total(0, h)
        send_p[0, h] = (xT[mine, part(h)].astype(F32) + gate_g * total).astype(BF)
    nzs = jnp.concatenate([dot_nt(own_sel, nv[:, pl.ds(w * 2 * SLICE, 2 * SLICE)]) for w in (0, 1)], axis=0)
    arrs = []
    for h in (0, 1):
        arr = sum(dot_nn(send_p[0, i], onehot[part(i), part(h)]) for i in (0, 1))
        arrs.append(arr)
        G[0, h, mine, :] = (alpha * arr + sigma * nzs[:, h * HALF:(h + 1) * HALF]).astype(BF)
        ag_first(0, h)
    for h in (0, 1):
        ag_second(0, h)
    have(TQ)
    have(FQ)
    biases = (dot_tn(cols_b, W[TQ])[3:4], dot_tn(cols_b, W[FQ])[6:7])

    for h in (0, 1):
        ag_wait(0, h)
        nf = G[0, h].astype(F32)
        rsend[h] = dot_nn(jnp.ones((8, QUARTER), BF), (nf * nf).astype(BF))
        for k in (2, 1, 3):
            y_send(YRR, k, rsend.at[h], rrecv.at[g, h], h)
        an[0, h] = (nf * (1.0 + colsT[:, 4:5])).astype(BF)
        an[1, h] = (nf * (1.0 + colsT[:, 7:8])).astype(BF)
        for n, k in ((0, TQ), (1, FQ)):
            to_bf_rows(qsc.at[n], dot_tn(an[n, h], W[k]), biases[n], h)
        for k in (2, 1, 3):
            t = others[k - 1]
            start_if(t != 0, rdma(q_message(qsc.at[t // 3], h), q_message(qbuf.at[g], h),
                                  YQC + 4 * h + k, YQC + 4 * h + g, group=t))
    start_if(g != 0, rdma(send_p.at[0], pbuf.at[g], YGN, YGN + g, group=0))
    have(TO)
    rn_rows = []
    for h in (0, 1):
        square = rsend[h]
        for o in others:
            y_wait(YRR, o, rrecv.at[o, h], h)
            square = square + rrecv[o, h]
        rn_rows.append(lax.rsqrt(square[0:1, :] * (1.0 / D) + EPSILON))
        crit_m = [rdma(mb.at[g, part(h)], mb.at[g, part(h)], YMC + 4 * h + k, YMC + 4 * h + g, group=others[k - 1])
                  for k in (2, 1, 3)]

        @pl.when(g != 0)
        def _():
            for o in others:
                y_wait(YQC, o, q_message(qbuf.at[o], h), h)
            r = jnp.transpose(jnp.broadcast_to(rn_rows[h], (128, HALF)))[:, 0:1]
            attend(r, qsc.at[g // 3], h)
            for copy in crit_m:
                copy.start()

        guarded.extend((g != 0, copy) for copy in crit_m)
    have(FO)
    for h in (0, 1):
        for r in (1, 2, 3):
            @pl.when(g != r)
            def _():
                y_wait(YMC, r, mb.at[r, part(h)], h)
            planes(r, TO if r < 3 else FO, mb.at[r], h)
            rs_first(r, h)
        for r in (1, 2, 3):
            rs_second(r, h)

    dist = jnp.zeros((1, HALF), F32)
    for h in (0, 1):
        own_n = G[0, h, mine, :].astype(F32)
        preds = []
        for r in (1, 2, 3):
            gate = gate_t if r < 3 else gate_f
            send_p[r, h] = (own_n + gate * rs_total(r, h)).astype(BF)
            preds.append(send_p[r, h].astype(F32))
        cond, uncond, faked = preds
        real = GUIDANCE * cond - (GUIDANCE - 1.0) * uncond
        score = faked - real
        fake_cot = faked - arrs[h]
        G[2, h, mine, :] = (gate_t * score).astype(BF)
        ag_first(2, h)
        G[3, h, mine, :] = (gate_f * fake_cot).astype(BF)
        ag_first(3, h)
        cots[1, h] = score
        cots[2, h] = fake_cot
        dist = dist + jnp.sum(jnp.abs(arrs[h] - real), axis=0, keepdims=True)
    for h in (0, 1):
        gen_cot = sum(dot_nt(cots[1, i].astype(BF), onehot[part(h), part(i)]) for i in (0, 1))
        cots[0, h] = gen_cot
        G[1, h, mine, :] = (gate_g * gen_cot).astype(BF)
        ag_first(1, h)
    dsend[0] = jnp.broadcast_to(dist, (8, 128))

    def butterfly(step):
        where = [dict(mp=m_core), dict(mp=m_x), dict(seq=s_x), dict(seq=s_pair), dict(seq=s_far)][step]
        return rdma(dsend.at[step], drecv.at[step], BUT + step, BUT + step, **where)

    def butterfly_end(step):
        rdma(drecv.at[step], drecv.at[step], BUT + step, BUT + step, mp=m_core).wait_recv()
        dsend[step + 1] = dsend[step] + drecv[step]

    start(butterfly(0))
    for h in (0, 1):
        for r in (2, 3):
            ag_second(r, h)
    for h in (0, 1):
        for r, k in ((2, TO), (3, FO)):
            ag_wait(r, h)
            gms[r - 1, part(h), :] = dot_tn(G[r, h], W[k]).astype(BF)
        for k in (2, 1, 3):
            t = others[k - 1]
            start_if(t != 0, rdma(gms.at[(t + 1) // 2, part(h)], gmb.at[g, part(h)],
                                  YGM + 4 * h + k, YGM + 4 * h + g, group=t))
        ag_second(1, h)
    for h in (0, 1):
        ag_wait(1, h)
        gms[0, part(h), :] = dot_tn(G[1, h], W[GO]).astype(BF)
        start_if(g != 0, rdma(gms.at[0, part(h)], gmb.at[g, part(h)], YGM + 4 * h, YGM + 4 * h + g, group=0))
    for k in (2, 1, 3):
        t = others[k - 1]
        start_if(t != 0, rdma(send_p.at[t], pbuf.at[g], YPR + k, YPR + g, group=t))
    butterfly_end(0)
    start(butterfly(1))

    factor = jnp.where(g == 1, -GUIDANCE, jnp.where(g == 2, GUIDANCE - 1.0, 1.0)).astype(F32)
    for h in (0, 1):
        tokens = part(h)
        for o in others:
            y_wait(YGM, o, gmb.at[o, tokens], h)
        total = gms[(g + 1) // 2, tokens, :].astype(F32)
        for o in others:
            total = total + gmb[o, tokens, :].astype(F32)
        gmb[g, tokens, :] = (total * factor).astype(BF)
        inner = jnp.zeros((HALF, 1), F32)
        for n in range(HEADS):
            lanes = pl.ds(n * HEAD, HEAD)
            qh = qq[tokens, lanes]
            rq = lax.rsqrt(jnp.mean(qh * qh, axis=1, keepdims=True) + EPSILON)
            unit = qh * rq
            w = probs[n, tokens, :].astype(F32)
            dp = dot_nt(gmb[g, tokens, lanes], values[:, lanes])
            gs = (w * (dp - jnp.sum(w * dp, axis=1, keepdims=True))).astype(BF)
            dqn = dot_nn(gs, keys[:, lanes]) * scaling
            grad = rq * (dqn - unit * jnp.mean(unit * dqn, axis=1, keepdims=True))
            gq[g, tokens, lanes] = grad.astype(BF)
            inner = inner + jnp.sum(grad * qA[tokens, lanes], axis=1, keepdims=True)
        for k in (2, 1, 3):
            y_send(YGQ, k, gq.at[g, tokens], gq.at[g, tokens], h)
        isend[0, :, part(h)] = jnp.transpose(jnp.broadcast_to(inner, (HALF, 128)))[0:8, :]
    start(rdma(isend.at[0], irecv.at[0], INN, INN, mp=m_core))
    butterfly_end(1)
    start(butterfly(2))

    def back_planes(r, h):
        @pl.when(g != r)
        def _():
            y_wait(YGQ, r, gq.at[r, part(h)], h)
        planes(4 + r, (GQ, TQ, TQ, FQ)[r], gq.at[r], h)
        rs_first(4 + r, h)

    def inner_and_distance(stage):
        if stage == 0:
            rdma(irecv.at[0], irecv.at[0], INN, INN, mp=m_core).wait_recv()
            isend[1] = isend[0] + irecv[0]
            start(rdma(isend.at[1], irecv.at[1], INN + 1, INN + 1, mp=m_x))
            butterfly_end(2)
            start(butterfly(3))
        if stage == 1:
            rdma(irecv.at[1], irecv.at[1], INN + 1, INN + 1, mp=m_x).wait_recv()
            irow[g] = isend[1] + irecv[1]
            for k in (2, 1, 3):
                y_send(YIN, k, irow.at[g], irow.at[g])
            butterfly_end(3)
            start(butterfly(4))
        if stage == 2:
            butterfly_end(4)
            for k in (2, 1, 3):
                y_send(YDI, k, dsend.at[5], drecv.at[5 + g])

    for h in (0, 1):
        for r in (1, 2, 3):
            back_planes(r, h)
        for r in (1, 2, 3):
            rs_second(4 + r, h)
        inner_and_distance(h)
    for h in (0, 1):
        back_planes(0, h)
    for h in (0, 1):
        rs_second(4, h)
    inner_and_distance(2)
    total = dsend[5]
    for o in others:
        y_wait(YDI, o, drecv.at[5 + o])
        total = total + drecv[5 + o]
    count = float(TOK * 16 // SAMPLES * D)
    inverse = 1.0 / (jnp.sum(total[0:1, :], axis=1, keepdims=True) * (1.0 / count) + FLOOR_EPSILON)
    for o in others:
        y_wait(YIN, o, irow.at[o])
    for r in (1, 2, 3, 0):
        scale = 1.0 + scols[:, (1, 4, 4, 7)[r]:(1, 4, 4, 7)[r] + 1]
        for h in (0, 1):
            rr = r1_row[:, h * HALF:(h + 1) * HALF] if r == 0 else rn_rows[h]
            rows = xT[mine, part(h)].astype(F32) if r == 0 else G[0, h, mine, :].astype(F32)
            ct = (1.0, -GUIDANCE, GUIDANCE - 1.0, 1.0)[r] * cots[(0, 1, 1, 2)[r], h]
            cube = rr * rr * rr * (irow[r][0:1, h * HALF:(h + 1) * HALF] * (1.0 / D))
            grads = ct + rr * scale * rs_total(4 + r, h) - rows * cube
            send_f[r, h] = (grads if r == 3 else grads * inverse).astype(BF)
            start_if(g != r, rdma(send_f.at[r, h], fbuf.at[g, h], YGH + 2 * r + h, YGH + 4 * h + g, group=r))
    pbuf[g] = send_p[g]
    fbuf[g] = send_f[g]

    def assemble(buf, w, h):
        rows = pl.ds(w * 2 * SUB, 2 * SUB)
        return sum(dot_tn(buf[o, h, rows, :], sel[o]) for o in range(4))

    @pl.when(g == 0)
    def _():
        for o in others:
            y_wait(YGN, o, pbuf.at[o])

    @pl.when(g != 0)
    def _():
        for o in others:
            y_wait(YPR, o, pbuf.at[o])

    windows = [pl.ds(w * 2 * SLICE, 2 * SLICE) for w in (0, 1)]
    for h in (0, 1):
        for w in (0, 1):
            out_p[0, part(h), windows[w]] = assemble(pbuf, w, h).astype(BF)
    for h in (0, 1):
        for o in others:
            y_wait(YGH, o, fbuf.at[o, h], h)
        for w in (0, 1):
            out_g[0, part(h), windows[w]] = assemble(fbuf, w, h)

    for cond, copy in guarded:
        @pl.when(cond)
        def _():
            copy.wait_send()

    for copy in pending:
        copy.wait_send()


def on_device(*operands):
    vmem = pl.BlockSpec(memory_space=pltpu.VMEM)
    smem = pl.BlockSpec(memory_space=pltpu.SMEM)
    hbm = pl.BlockSpec(memory_space=pl.ANY)
    act = lambda *lead: pltpu.VMEM(lead + (2, SLICE, HALF), BF)
    quarter = lambda lead: pltpu.VMEM((lead, 2, QUARTER, HALF), BF)
    (gen_input, noise, gen_steps, critic_steps, row_order) = operands[:5]
    tables = [tab.transpose(1, 0, 2) for tab in operands[11:14]]
    table = pltpu.VMEM(tables[0].shape, BF)
    return pl.pallas_call(
        kernel,
        out_shape=[
            jax.ShapeDtypeStruct((1, TOK, QUARTER), BF),
            jax.ShapeDtypeStruct((1, TOK, QUARTER), F32),
        ],
        in_specs=[smem, smem, vmem] + [hbm] * 13,
        out_specs=[vmem] * 2,
        scratch_shapes=[
            pltpu.VMEM((6, QUARTER, COLS), BF),
            pltpu.VMEM((QROWS, COLS), BF),
            pltpu.VMEM((2, QROWS, COLS), BF),
            pltpu.VMEM((4, QROWS, COLS), BF),
            pltpu.VMEM((TOK, COLS), F32),
            pltpu.VMEM((TOK, COLS), F32),
            pltpu.VMEM((HEADS, TOK, TEXT), BF),
            pltpu.VMEM((4, TOK, COLS), BF),
            quarter(8),
            pltpu.VMEM((8, 2, 2, SLICE, HALF), BF),
            act(8),
            act(8),
            quarter(4),
            quarter(2),
            pltpu.VMEM((TOK, D), BF),
            pltpu.VMEM((TOK, QUARTER), BF),
            table,
            table,
            table,
            pltpu.VMEM((TEXT, COLS), BF),
            pltpu.VMEM((TEXT, COLS), BF),
            pltpu.VMEM((TEXT, COLS), BF),
            pltpu.VMEM((16, D), BF),
            pltpu.VMEM((4, 2 * SUB, 2 * SLICE), BF),
            pltpu.VMEM((QUARTER, TOK), BF),
            pltpu.VMEM((TOK, TOK), BF),
            pltpu.VMEM((QUARTER, 16), F32),
            act(4),
            act(4),
            act(4),
            act(4),
            pltpu.VMEM((3, 2, SLICE, HALF), F32),
            pltpu.VMEM((3, TOK, COLS), BF),
            pltpu.VMEM((4, TOK, COLS), BF),
            pltpu.VMEM((4, TOK, COLS), BF),
            pltpu.VMEM((2, 8, HALF), F32),
            pltpu.VMEM((4, 2, 8, HALF), F32),
            pltpu.VMEM((2, 8, TOK), F32),
            pltpu.VMEM((2, 8, TOK), F32),
            pltpu.VMEM((4, 8, TOK), F32),
            pltpu.VMEM((6, 8, 128), F32),
            pltpu.VMEM((9, 8, 128), F32),
            pltpu.SemaphoreType.DMA((N_SEM,)),
            pltpu.SemaphoreType.DMA((N_SEM,)),
            pltpu.SemaphoreType.DMA((13,)),
        ],
        compiler_params=pltpu.CompilerParams(
            collective_id=0, has_side_effects=True, vmem_limit_bytes=60 * 2**20
        ),
        cost_estimate=pl.CostEstimate(flops=8 * 10**9, bytes_accessed=10**7, transcendentals=10**6),
    )(gen_steps, critic_steps, row_order, gen_input, noise, *operands[5:11], *tables, *operands[14:])


def solution(mesh):
    placed = (
        P("seq", None),
        P("seq", None),
        P(),
        P(),
        P("seq", None),
        P("seq", "mp"),
        P("seq", "mp"),
        P("seq", "mp"),
        P("seq", "mp"),
        P("seq", "mp"),
        P("seq", "mp"),
        P(),
        P(),
        P(),
        P("group", None, "mp"),
        P("group", None, "mp"),
    )
    return jax.shard_map(
        on_device,
        mesh=mesh,
        in_specs=placed,
        out_specs=(P("group", "seq", "mp"), P("group", "seq", "mp")),
        check_vma=False,
    )
```

time: 256 us -> 206 us (0.80)
  Pallas kernels: 245 us -> 201 us
  local copies, waits for them, and re-layouts: 10.4 us -> 4.42 us
    pallas_call x1, Pallas kernels: 245 us -> 201 us  [on_device(): pl.pallas_call(kernel, out_shape=[jax.ShapeDtypeStruct((1, TOK, QUARTER),...]
    unnamed x7 -> x2, local copies, waits for them, and re-layouts: 10.4 us -> 4.42 us
where the time goes in v3:
time: 206 us
  Pallas kernels  201 us (98%)
  local copies, waits for them, and re-layouts  4.42 us (2%)
    pallas_call x1, Pallas kernels, on_device(): pl.pallas_call(kernel, out_shape=[jax.ShapeDtypeStruct((1, TOK, QUARTER),...  201 us
    unnamed x2, local copies, waits for them, and re-layouts  4.42 us

profile of v3, /device:TPU:2, one launch (start us, length us, event | category | flops | bytes accessed | tf_op | source)
XLA Modules:
  0.0 206.0 jit_solution(8554955608227050467)
XLA Ops:
  0.6 200.9 %shard_map.167 = (bf16[1,256,1280]{2,1,0:T(8,128)(2,1)}, f32[1,256,1280]{2,1,0:T(8,128)}) custom-call(s32[2]{0:T(128)} %gen_steps.1, s32[2]{0:T(128)} %critic_steps.1, s32[1,256]{1,0:T(1,128)} %row_order.1, bf16[256,5120]{1,0:T(8,128)(2,1)} %gen_input.1, bf16[256,5120]{1,0:T(8,128)(2,1)} %noise.1, bf16[320,640]{1,0:T(8,128)(2,1)} %w_gq.1, ...), custom_call_target="tpu_custom_call" | custom-call | flops 8000000000 | bytes 10000000 | tf_op jit(solution)/shard_map/pallas_call | solution.py:641
  201.6 2.0 copy.20
  203.5 2.5 %copy.21 = f32[1,256,1280]{2,1,0:T(8,128)} copy(f32[1,256,1280]{2,1,0:T(8,128)} %get-tuple-element.5) | data formatting | bytes 2621440

commit v4 on v3

--- a/solution.py
+++ b/solution.py
@@ -18,8 +18,9 @@
 QUARTER = 1280
 QROWS = TOK + 16
 HALF = 128
-RING_START = (0, 2, 4, 6, 8, 10)
-X_LAST = (False, True, False, True, False, True)
+RING_START = (0, 1, 2, 3, 4, 5)
+X_LAST = (True, False, True, False, True, False)
+RING_POLLS = (3, 4, 5, 5, 6)
 EPSILON = 1e-06
 FLOOR_EPSILON = 1e-05
 GUIDANCE = 3.0
@@ -77,10 +78,10 @@
 def kernel(
     gen_steps, critic_steps, row_order, gen_input, noise,
     w_gq, w_go, w_tq, w_to, w_fq, w_fo, tab_g, tab_t, tab_f, text_keys, text_values,
-    out_p, out_g,
+    pbuf, fbuf,
     W, qsg, qsc, qbuf, qA, qq, probs, mb, PP, CC, SS, XX, G, an,
-    xv, nv, tg, tt, tf, kraw, keys, values, modv, sel, xT, onehot, colsT,
-    send_p, send_f, pbuf, fbuf, cots, gms, gmb, gq, rsend, rrecv, isend, irecv, irow, dsend, drecv,
+    xv, nv, tg, tt, tf, kraw, keys, values, xT, onehot, colsT,
+    nzt, send_p, send_f, cots, gms, gmb, gq, rsend, rrecv, isend, irecv, irow, dsend, drecv,
     ssem, rsem, lsem,
 ):
     g = lax.axis_index("group")
@@ -123,15 +124,24 @@
         pltpu.make_async_copy(noise.at[:, mine_of_d], nv, lsem.at[6]),
     ]
 
+    def rows_of(zz, x):
+        return pl.ds(pl.multiple_of((lax.rem(zz + 16, 8) * 2 + x) * SUB, 16), SUB)
+
+    my_rows = rows_of(z, xh)
+    own_loads = [pltpu.make_async_copy(own_w[k], W.at[k, my_rows], lsem.at[7 + k]) for k in range(6)]
+    for copy in loads + own_loads:
+        copy.start()
+
     barrier = pltpu.get_barrier_semaphore()
     peers = [{"group": o} for o in others]
     peers += [{"mp": m_core}, {"mp": m_x}, {"seq": s_x}, {"seq": s_up}, {"seq": s_down}, {"seq": s_far}]
     for peer in peers:
         pl.semaphore_signal(barrier, inc=1, device_id=peer, device_id_type=pl.DeviceIdType.MESH)
+    row = lax.broadcasted_iota(jnp.int32, (2 * SUB, 2 * SLICE), 0)
+    col = lax.broadcasted_iota(jnp.int32, (2 * SUB, 2 * SLICE), 1)
+    base = row + jnp.where(row >= SUB, SLICE - SUB, 0)
+    own_sel = (col == base + g * SUB).astype(BF)
     pl.semaphore_wait(barrier, len(peers))
-
-    def rows_of(zz, x):
-        return pl.ds(pl.multiple_of((lax.rem(zz + 16, 8) * 2 + x) * SUB, 16), SUB)
 
     def steps_of(way, side):
         return 4 if way == side else 3
@@ -165,25 +175,30 @@
         sem = XCH + 8 * k + number
         rdma(W.at[k, rows], W.at[k, rows], sem, sem, seq=s_x).wait_recv()
 
-    my_rows = rows_of(z, xh)
-    own_loads = [pltpu.make_async_copy(own_w[k], W.at[k, my_rows], lsem.at[7 + k]) for k in range(6)]
-    for k in range(6):
-        if not X_LAST[k]:
-            x_send(k, 0, own_w[k], my_rows)
-
-    state = {"tick": 0, "begun": 0}
-
-    def ring_begin(tick):
+
+    state = {"tick": 0, "begun": 0, "sent": 0}
+
+    def x_ahead(last):
+        while state["sent"] <= min(last, 5):
+            if not X_LAST[state["sent"]]:
+                x_send(state["sent"], 0, own_w[state["sent"]], my_rows)
+            state["sent"] += 1
+
+    def ring_begin(tick, between=None):
         while state["begun"] < 6 and RING_START[state["begun"]] <= tick:
             k = state["begun"]
+            x_ahead(k)
             for way in (0, 1):
                 ring_send(k, way, 0, 0)
             if X_LAST[k]:
                 x_send(k, 0, own_w[k], my_rows)
-            else:
+            if between is not None:
+                between()
+            if not X_LAST[k]:
                 x_wait(k, 0, z)
                 for way in (0, 1):
                     ring_send(k, way, 1, 0)
+            x_ahead(k + 1)
             state["begun"] += 1
 
     def ring_to(last):
@@ -203,7 +218,8 @@
 
     def have(k):
         ring_to(RING_START[k] + 3)
-        own_loads[k].wait()
+        if k != GQ:
+            own_loads[k].wait()
         if X_LAST[k]:
             x_wait(k, 0, z)
             for t in range(4):
@@ -301,67 +317,74 @@
         if h == 0:
             ref[0:16, :] = jnp.broadcast_to(bias, (16, COLS)).astype(BF)
 
-    ring_begin(0)
-    for copy in loads + own_loads:
-        copy.start()
-    row = lax.broadcasted_iota(jnp.int32, (2 * SUB, 2 * SLICE), 0)
-    col = lax.broadcasted_iota(jnp.int32, (2 * SUB, 2 * SLICE), 1)
-    base = row + jnp.where(row >= SUB, SLICE - SUB, 0)
-    for o in range(4):
-        sel[o] = (col == base + o * SUB).astype(BF)
-    ring_to(0)
-    order = lax.broadcasted_iota(jnp.int32, (TOK, TOK), 0)
-    onehot[...] = (order == row_order[...]).astype(BF)
-    for copy in loads:
-        copy.wait()
-    picked = []
-    pr = lax.broadcasted_iota(jnp.int32, (16, 16), 0)
-    pc = lax.broadcasted_iota(jnp.int32, (16, 16), 1)
-    for n, (tab, step) in enumerate(((tg, gen_steps), (tt, critic_steps), (tf, critic_steps))):
-        for j in range(3):
-            hit = jnp.where(pr == 3 * n + j, (pc == step[sample]).astype(F32), 0.0).astype(BF)
-            picked.append(dot_nn(hit, tab[j]))
-    modv[...] = sum(picked).astype(BF)
-    ring_to(1)
-    own_sel = sel[g]
-    square_row = jnp.zeros((8, TOK), F32)
-    square_col = jnp.zeros((TOK, 128), F32)
-    for w in range(8):
+    table_row = lax.broadcasted_iota(jnp.int32, (16, 2 * SLICE), 0)
+
+    def prepare(w):
         window = pl.ds(w * 2 * SLICE, 2 * SLICE)
         rows = pl.ds(w * 2 * SUB, 2 * SUB)
-        piece = xv[:, window]
-        xw = dot_nt(own_sel, piece)
-        cw = dot_nt(own_sel, modv[:, window])
+        mods = jnp.zeros((16, 2 * SLICE), F32)
+        for n, (tab, step) in enumerate(((tg, gen_steps), (tt, critic_steps), (tf, critic_steps))):
+            for j in range(3):
+                value = jnp.where(table_row == step[sample], tab[j, :, window].astype(F32), 0.0)
+                value = jnp.sum(value, axis=0, keepdims=True)
+                mods = jnp.where(table_row == 3 * n + j, value, mods)
+        xw = dot_nt(own_sel, xv[:, window])
+        cw = dot_nt(own_sel, mods.astype(BF))
         colsT[rows, :] = cw
         xT[rows, :] = xw.astype(BF)
         axw = (xw * (1.0 + cw[:, 1:2])).astype(BF)
         for h in (0, 1):
             an[0, h, rows, :] = axw[:, h * HALF:(h + 1) * HALF]
-        sq = piece.astype(F32)
-        sq = (sq * sq).astype(BF)
-        square_row = square_row + dot_nt(jnp.ones((8, 2 * SLICE), BF), sq)
-        square_col = square_col + dot_nn(sq, jnp.ones((2 * SLICE, 128), BF))
-        if w == 3:
-            ring_to(2)
-    r1_row = lax.rsqrt(square_row[0:1, :] * (1.0 / D) + EPSILON)
-    r1 = lax.rsqrt(square_col[:, 0:1] * (1.0 / D) + EPSILON)
+
+    def prepare_first():
+        for copy in loads[:4]:
+            copy.wait()
+        prepare(0)
+        prepare(1)
+
+    ring_begin(0, prepare_first)
+    prepare(2)
+    prepare(3)
+    ring_to(0)
+    prepare(4)
+    prepare(5)
+    ring_to(1)
+    prepare(6)
+    prepare(7)
+    own_loads[GQ].wait()
+    cols_b = colsT[...].astype(BF)
+    mine = slice_rows(m)
+    scols = colsT[mine, :]
+    gate_g, gate_t, gate_f = scols[:, 2:3], scols[:, 5:6], scols[:, 8:9]
+
+    have(GQ)
+    bias = dot_tn(cols_b, W[GQ])[0:1]
+    for h in (0, 1):
+        to_bf_rows(qsg, dot_tn(an[0, h], W[GQ]), bias, h)
+        start_if(g != 0, rdma(q_message(qsg, h), q_message(qbuf.at[g], h), YQG + 4 * h, YQG + 4 * h + g, group=0))
+    ring_to(RING_POLLS[0])
+    order = lax.broadcasted_iota(jnp.int32, (TOK, TOK), 0)
+    onehot[...] = (order == row_order[...]).astype(BF)
+    for copy in loads[4:]:
+        copy.wait()
     for n in range(HEADS):
         lanes = pl.ds(n * HEAD, HEAD)
         kf = kraw[:, lanes].astype(F32)
         keys[:, lanes] = (kf * lax.rsqrt(jnp.mean(kf * kf, axis=1, keepdims=True) + EPSILON)).astype(BF)
-    cols_b = colsT[...].astype(BF)
-    mine = slice_rows(m)
-    scols = colsT[mine, :]
-    gate_g, gate_t, gate_f = scols[:, 2:3], scols[:, 5:6], scols[:, 8:9]
+    square_row = jnp.zeros((8, TOK), F32)
+    square_col = jnp.zeros((TOK, 128), F32)
+    for w in range(8):
+        sq = xv[:, pl.ds(w * 2 * SLICE, 2 * SLICE)].astype(F32)
+        sq = (sq * sq).astype(BF)
+        square_row = square_row + dot_nt(jnp.ones((8, 2 * SLICE), BF), sq)
+        square_col = square_col + dot_nn(sq, jnp.ones((2 * SLICE, 128), BF))
+    r1_row = lax.rsqrt(square_row[0:1, :] * (1.0 / D) + EPSILON)
+    r1 = lax.rsqrt(square_col[:, 0:1] * (1.0 / D) + EPSILON)
     angle = jnp.full((8, 128), critic_steps[sample] + 1).astype(F32) * (0.5 * 3.141592653589793 / (tg.shape[1] + 1.0))
     alpha, sigma = jnp.cos(angle)[0:1, 0:1], jnp.sin(angle)[0:1, 0:1]
-
-    have(GQ)
-    bias = dot_tn(cols_b, W[GQ])[0:1]
-    for h in (0, 1):
-        to_bf_rows(qsg, dot_tn(an[0, h], W[GQ]), bias, h)
-        start_if(g != 0, rdma(q_message(qsg, h), q_message(qbuf.at[g], h), YQG + 4 * h, YQG + 4 * h + g, group=0))
-    ring_to(RING_START[GO] + 3)
+    nzs = jnp.concatenate([dot_nt(own_sel, nv[:, pl.ds(w * 2 * SLICE, 2 * SLICE)]) for w in (0, 1)], axis=0)
+    nzt[...] = sigma * nzs
+    ring_to(RING_POLLS[1])
 
     gen_m = []
     for h in (0, 1):
@@ -379,7 +402,7 @@
 
     guarded.extend((g == 0, copy) for copy in gen_m)
     have(GO)
-    ring_to(RING_START[TQ] + 3)
+    ring_to(RING_POLLS[2])
     for h in (0, 1):
         @pl.when(g != 0)
         def _():
@@ -388,19 +411,19 @@
         rs_first(0, h)
     for h in (0, 1):
         rs_second(0, h)
-    ring_to(RING_START[FQ] + 3)
+    ring_to(RING_POLLS[3])
     for h in (0, 1):
         total = rs_total(0, h)
         send_p[0, h] = (xT[mine, part(h)].astype(F32) + gate_g * total).astype(BF)
-    nzs = jnp.concatenate([dot_nt(own_sel, nv[:, pl.ds(w * 2 * SLICE, 2 * SLICE)]) for w in (0, 1)], axis=0)
     arrs = []
     for h in (0, 1):
         arr = sum(dot_nn(send_p[0, i], onehot[part(i), part(h)]) for i in (0, 1))
         arrs.append(arr)
-        G[0, h, mine, :] = (alpha * arr + sigma * nzs[:, h * HALF:(h + 1) * HALF]).astype(BF)
+        G[0, h, mine, :] = (alpha * arr + nzt[:, part(h)]).astype(BF)
         ag_first(0, h)
     for h in (0, 1):
         ag_second(0, h)
+    ring_to(RING_POLLS[4])
     have(TQ)
     have(FQ)
     biases = (dot_tn(cols_b, W[TQ])[3:4], dot_tn(cols_b, W[FQ])[6:7])
@@ -465,9 +488,10 @@
         score = faked - real
         fake_cot = faked - arrs[h]
         G[2, h, mine, :] = (gate_t * score).astype(BF)
-        ag_first(2, h)
         G[3, h, mine, :] = (gate_f * fake_cot).astype(BF)
-        ag_first(3, h)
+        if h == 0:
+            ag_first(2, 0)
+            ag_first(3, 0)
         cots[1, h] = score
         cots[2, h] = fake_cot
         dist = dist + jnp.sum(jnp.abs(arrs[h] - real), axis=0, keepdims=True)
@@ -476,6 +500,8 @@
         cots[0, h] = gen_cot
         G[1, h, mine, :] = (gate_g * gen_cot).astype(BF)
         ag_first(1, h)
+    ag_first(2, 1)
+    ag_first(3, 1)
     dsend[0] = jnp.broadcast_to(dist, (8, 128))
 
     def butterfly(step):
@@ -487,10 +513,7 @@
         dsend[step + 1] = dsend[step] + drecv[step]
 
     start(butterfly(0))
-    for h in (0, 1):
-        for r in (2, 3):
-            ag_second(r, h)
-    for h in (0, 1):
+    def critics_back(h):
         for r, k in ((2, TO), (3, FO)):
             ag_wait(r, h)
             gms[r - 1, part(h), :] = dot_tn(G[r, h], W[k]).astype(BF)
@@ -498,14 +521,17 @@
             t = others[k - 1]
             start_if(t != 0, rdma(gms.at[(t + 1) // 2, part(h)], gmb.at[g, part(h)],
                                   YGM + 4 * h + k, YGM + 4 * h + g, group=t))
-        ag_second(1, h)
+
+    for r, h in ((2, 0), (3, 0), (1, 0), (1, 1)):
+        ag_second(r, h)
+    critics_back(0)
     for h in (0, 1):
         ag_wait(1, h)
         gms[0, part(h), :] = dot_tn(G[1, h], W[GO]).astype(BF)
         start_if(g != 0, rdma(gms.at[0, part(h)], gmb.at[g, part(h)], YGM + 4 * h, YGM + 4 * h + g, group=0))
-    for k in (2, 1, 3):
-        t = others[k - 1]
-        start_if(t != 0, rdma(send_p.at[t], pbuf.at[g], YPR + k, YPR + g, group=t))
+    for r in (2, 3):
+        ag_second(r, 1)
+    critics_back(1)
     butterfly_end(0)
     start(butterfly(1))
 
@@ -565,15 +591,14 @@
                 y_send(YDI, k, dsend.at[5], drecv.at[5 + g])
 
     for h in (0, 1):
-        for r in (1, 2, 3):
+        for r in (1, 2, 3, 0):
             back_planes(r, h)
-        for r in (1, 2, 3):
+        for r in (1, 2, 3, 0):
             rs_second(4 + r, h)
         inner_and_distance(h)
-    for h in (0, 1):
-        back_planes(0, h)
-    for h in (0, 1):
-        rs_second(4, h)
+    for k in (2, 1, 3):
+        t = others[k - 1]
+        start_if(t != 0, rdma(send_p.at[t], pbuf.at[g], YPR + k, YPR + g, group=t))
     inner_and_distance(2)
     total = dsend[5]
     for o in others:
@@ -583,22 +608,17 @@
     inverse = 1.0 / (jnp.sum(total[0:1, :], axis=1, keepdims=True) * (1.0 / count) + FLOOR_EPSILON)
     for o in others:
         y_wait(YIN, o, irow.at[o])
-    for r in (1, 2, 3, 0):
+    for h, r in [(h, r) for h in (0, 1) for r in (1, 2, 3, 0)]:
         scale = 1.0 + scols[:, (1, 4, 4, 7)[r]:(1, 4, 4, 7)[r] + 1]
-        for h in (0, 1):
-            rr = r1_row[:, h * HALF:(h + 1) * HALF] if r == 0 else rn_rows[h]
-            rows = xT[mine, part(h)].astype(F32) if r == 0 else G[0, h, mine, :].astype(F32)
-            ct = (1.0, -GUIDANCE, GUIDANCE - 1.0, 1.0)[r] * cots[(0, 1, 1, 2)[r], h]
-            cube = rr * rr * rr * (irow[r][0:1, h * HALF:(h + 1) * HALF] * (1.0 / D))
-            grads = ct + rr * scale * rs_total(4 + r, h) - rows * cube
-            send_f[r, h] = (grads if r == 3 else grads * inverse).astype(BF)
-            start_if(g != r, rdma(send_f.at[r, h], fbuf.at[g, h], YGH + 2 * r + h, YGH + 4 * h + g, group=r))
+        rr = r1_row[:, h * HALF:(h + 1) * HALF] if r == 0 else rn_rows[h]
+        rows = xT[mine, part(h)].astype(F32) if r == 0 else G[0, h, mine, :].astype(F32)
+        ct = (1.0, -GUIDANCE, GUIDANCE - 1.0, 1.0)[r] * cots[(0, 1, 1, 2)[r], h]
+        cube = rr * rr * rr * (irow[r][0:1, h * HALF:(h + 1) * HALF] * (1.0 / D))
+        grads = ct + rr * scale * rs_total(4 + r, h) - rows * cube
+        send_f[r, h] = (grads if r == 3 else grads * inverse).astype(BF)
+        start_if(g != r, rdma(send_f.at[r, h], fbuf.at[g, h], YGH + 2 * r + h, YGH + 4 * h + g, group=r))
     pbuf[g] = send_p[g]
     fbuf[g] = send_f[g]
-
-    def assemble(buf, w, h):
-        rows = pl.ds(w * 2 * SUB, 2 * SUB)
-        return sum(dot_tn(buf[o, h, rows, :], sel[o]) for o in range(4))
 
     @pl.when(g == 0)
     def _():
@@ -610,15 +630,9 @@
         for o in others:
             y_wait(YPR, o, pbuf.at[o])
 
-    windows = [pl.ds(w * 2 * SLICE, 2 * SLICE) for w in (0, 1)]
-    for h in (0, 1):
-        for w in (0, 1):
-            out_p[0, part(h), windows[w]] = assemble(pbuf, w, h).astype(BF)
     for h in (0, 1):
         for o in others:
             y_wait(YGH, o, fbuf.at[o, h], h)
-        for w in (0, 1):
-            out_g[0, part(h), windows[w]] = assemble(fbuf, w, h)
 
     for cond, copy in guarded:
         @pl.when(cond)
@@ -627,6 +641,15 @@
 
     for copy in pending:
         copy.wait_send()
+
+
+def assemble(p_ref, f_ref, out_p, out_g):
+    row = lax.broadcasted_iota(jnp.int32, (2 * SUB, 2 * SLICE), 0)
+    col = lax.broadcasted_iota(jnp.int32, (2 * SUB, 2 * SLICE), 1)
+    base = row + jnp.where(row >= SUB, SLICE - SUB, 0)
+    sel = [(col == base + o * SUB).astype(BF) for o in range(4)]
+    out_p[0] = sum(dot_tn(p_ref[o, 0], sel[o]) for o in range(4)).astype(BF)
+    out_g[0] = sum(dot_tn(f_ref[o, 0], sel[o]) for o in range(4))
 
 
 def on_device(*operands):
@@ -638,11 +661,11 @@
     (gen_input, noise, gen_steps, critic_steps, row_order) = operands[:5]
     tables = [tab.transpose(1, 0, 2) for tab in operands[11:14]]
     table = pltpu.VMEM(tables[0].shape, BF)
-    return pl.pallas_call(
+    predictions, grads = pl.pallas_call(
         kernel,
         out_shape=[
-            jax.ShapeDtypeStruct((1, TOK, QUARTER), BF),
-            jax.ShapeDtypeStruct((1, TOK, QUARTER), F32),
+            jax.ShapeDtypeStruct((4, 2, SLICE, HALF), BF),
+            jax.ShapeDtypeStruct((4, 2, SLICE, HALF), BF),
         ],
         in_specs=[smem, smem, vmem] + [hbm] * 13,
         out_specs=[vmem] * 2,
@@ -669,13 +692,10 @@
             pltpu.VMEM((TEXT, COLS), BF),
             pltpu.VMEM((TEXT, COLS), BF),
             pltpu.VMEM((TEXT, COLS), BF),
-            pltpu.VMEM((16, D), BF),
-            pltpu.VMEM((4, 2 * SUB, 2 * SLICE), BF),
             pltpu.VMEM((QUARTER, TOK), BF),
             pltpu.VMEM((TOK, TOK), BF),
             pltpu.VMEM((QUARTER, 16), F32),
-            act(4),
-            act(4),
+            pltpu.VMEM((SLICE, TOK), F32),
             act(4),
             act(4),
             pltpu.VMEM((3, 2, SLICE, HALF), F32),
@@ -698,6 +718,16 @@
         ),
         cost_estimate=pl.CostEstimate(flops=8 * 10**9, bytes_accessed=10**7, transcendentals=10**6),
     )(gen_steps, critic_steps, row_order, gen_input, noise, *operands[5:11], *tables, *operands[14:])
+    return pl.pallas_call(
+        assemble,
+        grid=(2, 2),
+        out_shape=[
+            jax.ShapeDtypeStruct((1, TOK, QUARTER), BF),
+            jax.ShapeDtypeStruct((1, TOK, QUARTER), F32),
+        ],
+        in_specs=[pl.BlockSpec((4, 1, 2 * SUB, HALF), lambda h, w: (0, h, w, 0))] * 2,
+        out_specs=[pl.BlockSpec((1, HALF, 2 * SLICE), lambda h, w: (0, h, w))] * 2,
+    )(predictions, grads)
 
 
 def solution(mesh):

time: 206 us -> 198 us (0.961); the launches traced: 206 us -> 196 us
  Pallas kernels: 201 us -> 195 us
  local copies, waits for them, and re-layouts: 4.42 us -> 0 us
    pallas_call x1 -> x2, Pallas kernels: 201 us -> 195 us  [the longest x1 190 us: on_device(): pl.pallas_call(kernel, out_shape=[jax.ShapeDtypeStruct((4, 2, SLICE, HALF...]
    unnamed x2 -> x0, local copies, waits for them, and re-layouts: 4.42 us -> none
where the time goes in v4:
time: 198 us; the launch traced here: 196 us
  Pallas kernels  195 us (98%)
    pallas_call x1, Pallas kernels, on_device(): pl.pallas_call(kernel, out_shape=[jax.ShapeDtypeStruct((4, 2, SLICE, HALF...  190 us
    pallas_call x1, Pallas kernels, on_device(): pl.pallas_call(assemble, grid=(2, 2), out_shape=[jax.ShapeDtypeStruct((1,...  4.81 us

profile of v4, /device:TPU:2, one launch (start us, length us, event | category | flops | bytes accessed | tf_op | source)
XLA Modules:
  0.0 195.9 jit_solution(17264584332094690774)
XLA Ops:
  0.6 190.5 %shard_map.167 = (bf16[4,2,320,128]{3,2,1,0:T(8,128)(2,1)}, bf16[4,2,320,128]{3,2,1,0:T(8,128)(2,1)}) custom-call(s32[2]{0:T(128)} %gen_steps.1, s32[2]{0:T(128)} %critic_steps.1, s32[1,256]{1,0:T(1,128)} %row_order.1, bf16[256,5120]{1,0:T(8,128)(2,1)} %gen_input.1, bf16[256,5120]{1,0:T(8,128)(2,1)} %noise.1, bf16[320,640]{1,0:T(8,128)(2,1)} %w_gq.1, ...), custom_call_target="tpu_custom_call" | custom-call | flops 8000000000 | bytes 10000000 | tf_op jit(solution)/shard_map/pallas_call | solution.py:664
  191.1 4.8 %shard_map.168 = (bf16[1,256,1280]{2,1,0:T(8,128)(2,1)}, f32[1,256,1280]{2,1,0:T(8,128)}) custom-call(bf16[4,2,320,128]{3,2,1,0:T(8,128)(2,1)} %get-tuple-element.4.p_ref, bf16[4,2,320,128]{3,2,1,0:T(8,128)(2,1)} %get-tuple-element.5.f_ref), custom_call_target="tpu_custom_call" | custom-call | tf_op jit(solution)/shard_map/pallas_call | solution.py:721

commit v5 on v4

--- a/solution.py
+++ b/solution.py
@@ -443,7 +443,7 @@
             start_if(t != 0, rdma(q_message(qsc.at[t // 3], h), q_message(qbuf.at[g], h),
                                   YQC + 4 * h + k, YQC + 4 * h + g, group=t))
     start_if(g != 0, rdma(send_p.at[0], pbuf.at[g], YGN, YGN + g, group=0))
-    have(TO)
+    ring_to(RING_START[TO] + 3)
     rn_rows = []
     for h in (0, 1):
         square = rsend[h]
@@ -464,6 +464,7 @@
                 copy.start()
 
         guarded.extend((g != 0, copy) for copy in crit_m)
+    have(TO)
     have(FO)
     for h in (0, 1):
         for r in (1, 2, 3):

time: 198 us -> 198 us (level)
  no operation moved by 1% of the time
where the time goes in v5:
time: 198 us; the launch traced here: 196 us
  Pallas kernels  195 us (98%)
    pallas_call x1, Pallas kernels, on_device(): pl.pallas_call(kernel, out_shape=[jax.ShapeDtypeStruct((4, 2, SLICE, HALF...  190 us
    pallas_call x1, Pallas kernels, on_device(): pl.pallas_call(assemble, grid=(2, 2), out_shape=[jax.ShapeDtypeStruct((1,...  4.82 us

profile of v5, /device:TPU:2, one launch (start us, length us, event | category | flops | bytes accessed | tf_op | source)
XLA Modules:
  0.0 195.9 jit_solution(5195123253537515636)
XLA Ops:
  0.6 190.5 %shard_map.167 = (bf16[4,2,320,128]{3,2,1,0:T(8,128)(2,1)}, bf16[4,2,320,128]{3,2,1,0:T(8,128)(2,1)}) custom-call(s32[2]{0:T(128)} %gen_steps.1, s32[2]{0:T(128)} %critic_steps.1, s32[1,256]{1,0:T(1,128)} %row_order.1, bf16[256,5120]{1,0:T(8,128)(2,1)} %gen_input.1, bf16[256,5120]{1,0:T(8,128)(2,1)} %noise.1, bf16[320,640]{1,0:T(8,128)(2,1)} %w_gq.1, ...), custom_call_target="tpu_custom_call" | custom-call | flops 8000000000 | bytes 10000000 | tf_op jit(solution)/shard_map/pallas_call | solution.py:665
  191.1 4.8 %shard_map.168 = (bf16[1,256,1280]{2,1,0:T(8,128)(2,1)}, f32[1,256,1280]{2,1,0:T(8,128)}) custom-call(bf16[4,2,320,128]{3,2,1,0:T(8,128)(2,1)} %get-tuple-element.4.p_ref, bf16[4,2,320,128]{3,2,1,0:T(8,128)(2,1)} %get-tuple-element.5.f_ref), custom_call_target="tpu_custom_call" | custom-call | tf_op jit(solution)/shard_map/pallas_call | solution.py:722
